TPU v7x, 32 devices: a whole 2x2x4 slice. The times are simulated.
32 devices in a mesh: seq: 8 (over z, x), tp: 4 (over y, core).
Axes of the slice: x: 2, y: 2, z: 4, core: 2. Of those that a mesh axis runs over, the one named last changes fastest.
Arguments:
- layer_input: bfloat16 [2, 4096, 768], P(None, 'seq'), may hold values from -8 to 8
- out_grad: bfloat16 [2, 4096, 768], P(None, 'seq'), may hold values from -6 to 6
- norm1_gain: float32 [768], replicated, may hold values from 0.5 to 1.5
- norm1_shift: float32 [768], replicated, may hold values from -1 to 1
- w_qkv: bfloat16 [768, 3, 768], P(None, None, 'tp'), may hold values from -0.21875 to 0.21875
- w_out: bfloat16 [768, 768], P(None, 'tp'), may hold values from -0.875 to 0.875
- norm2_gain: float32 [768], replicated, may hold values from 0.5 to 1.5
- norm2_shift: float32 [768], replicated, may hold values from -1 to 1
- w_up: bfloat16 [768, 3072], P(None, 'tp'), may hold values from -0.21875 to 0.21875
- w_down: bfloat16 [768, 3072], P(None, 'tp'), may hold values from -0.21875 to 0.21875
- key_keep: int32 [2, 4096], replicated, may hold values from 0 to 1, as said below
- rand_blocks: int32 [2, 64, 3], replicated, may hold values from 0 to 63, as said below
Outputs:
- layer_output: float32 [2, 4096, 768], P(None, ('seq', 'tp'))
- input_grad: float32 [2, 4096, 768], P(None, ('seq', 'tp'))
- grad_w_qkv: float32 [768, 3, 768], P('seq', None, 'tp')
- grad_w_out: float32 [768, 768], P('seq', 'tp')
- grad_w_up: float32 [768, 3072], P('seq', 'tp')
- grad_w_down: float32 [768, 3072], P('seq', 'tp')
- grad_norm1_gain: float32 [768], P('seq')
- grad_norm1_shift: float32 [768], P('seq')
- grad_norm2_gain: float32 [768], P('seq')
- grad_norm2_shift: float32 [768], P('seq')
Inputs may be any that keep to these rules, and one draw needn't show every extreme that they name: `key_keep`: in every block of 64 positions the kept positions come first, 16 or more of them. `rand_blocks`: entry [m, b, j] names a key block of sequence m. Over all 2 sequences, the random blocks of the query blocks held by one index of seq lie on any one index at most 6 times, and exactly 6 times on some index.
All inputs are finite; a program needn't handle non-finite values.
Results may differ from a plain program's by a relative error of at most 0.012.
Values may be sent and summed in bfloat16 or wider, within the bound.
No kernel may reach another device: no remote copies, remote signals or barrier semaphores. Data moves between devices by JAX's collectives and lax.ppermute only.
A program may use at most 384 MiB of HBM per device.

v0:
```python
from functools import partial
import math

import jax
import jax.numpy as jnp
from jax import lax
from jax.experimental import pallas as pl
from jax.experimental.pallas import tpu as pltpu
from jax.sharding import PartitionSpec as P

HD = 64
BLOCK = 64
RANDS = 3
EPS = 1e-06
SWAP = (0, 2, 1, 3)
NEG = -1e30
Q_LANES = (128, 192, 0)
O_LANES = (0, 64, 192)
K_PART = slice(128, 384)
V_PART = slice(0, 256)
F32 = jnp.float32
BF16 = jnp.bfloat16
VMEM = pl.BlockSpec(memory_space=pltpu.VMEM)
SMEM = pl.BlockSpec(memory_space=pltpu.SMEM)
MIB = 1024 * 1024


def sds(shape, kind):
    return jax.ShapeDtypeStruct(shape, kind)


PARAMS = pltpu.CompilerParams(vmem_limit_bytes=56 * MIB)
SMALL = pltpu.CompilerParams(vmem_limit_bytes=12 * MIB)
MIDDLE = pltpu.CompilerParams(vmem_limit_bytes=24 * MIB)


def after(value, *others):
    return lax.optimization_barrier((value,) + others)[0]


class Chain:
    last = ()

    def link(self, value):
        return after(value, *self.last) if self.last else value

    def done(self, outs):
        self.last = (jax.tree.leaves(outs)[0],)
        return outs


CHAIN = Chain()


def part_of(array, at, count):
    return array, at, count


TIMES = {
    "project": 6, "dispatch": 3, "bias": 2, "lead_fwd": 4, "sparse_fwd": 7, "merge": 1, "lead_finish": 1, "out_project": 1,
    "mid_fwd": 1, "gather": 2, "ffn": 6, "ffn_grad": 7, "mid_bwd": 1, "heads_grad": 5, "lead_grad": 1, "sparse_bwd": 13,
    "fold_near": 3, "down": 6, "lead_bwd": 5, "slots": 14, "tail": 5, "fold_far": 2, "back": 7, "output": 1,
    "fold": 2, "end": 2,
}
HINT = 1.75e6


def cost(name):
    return pl.CostEstimate(flops=0, transcendentals=0, bytes_accessed=int(TIMES[name] * HINT))


def call(body, outs, scratch=(), name=None, limit=PARAMS):
    def run(*args, smem=()):
        specs = [SMEM] * len(smem)
        arrays = []
        if smem:
            smem = (CHAIN.link(smem[0]),) + tuple(smem[1:])
        else:
            args = (CHAIN.link(args[0]),) + args[1:]
        for arg in args:
            if isinstance(arg, tuple):
                array, at, count = arg
                shape = (array.shape[0] // count,) + array.shape[1:]
                index = (at,) + (0,) * (array.ndim - 1)
                specs.append(pl.BlockSpec(shape, lambda i, index=index: index))
                arrays.append(array)
            else:
                specs.append(VMEM)
                arrays.append(arg)
        return CHAIN.done(
            pl.pallas_call(
                body,
                out_shape=outs,
                grid=(1,),
                in_specs=specs,
                out_specs=jax.tree.map(lambda _: VMEM, outs),
                scratch_shapes=list(scratch),
                compiler_params=limit,
                cost_estimate=cost(name),
                name=name,
            )(*smem, *arrays)
        )

    return run


def share_call(body, outs, blocks, name, limit=SMALL):
    def run(meta, seqs, share, *args):
        def spec(value, group, pos):
            return pl.BlockSpec(
                (seqs, share, value.shape[2]), lambda i, meta_ref: (group, meta_ref[0] ^ SWAP[pos], 0)
            )

        return CHAIN.done(
            pl.pallas_call(
                body,
                out_shape=outs,
                grid_spec=pltpu.PrefetchScalarGridSpec(
                    num_scalar_prefetch=1,
                    grid=(1,),
                    in_specs=[spec(*b) for b in blocks] + [VMEM] * len(args),
                    out_specs=jax.tree.map(lambda _: VMEM, outs),
                ),
                compiler_params=limit,
                cost_estimate=cost(name),
                name=name,
            )(CHAIN.link(meta), *(b[0] for b in blocks), *args)
        )

    return run


def dot_nt(a, b):
    return lax.dot_general(a, b, (((1,), (1,)), ((), ())), preferred_element_type=F32)


def dot_tn(a, b):
    return lax.dot_general(a, b, (((0,), (0,)), ((), ())), preferred_element_type=F32)


def dot_nn(a, b):
    return lax.dot_general(a, b, (((1,), (0,)), ((), ())), preferred_element_type=F32)


def stack(rows, lanes):
    lane = lax.broadcasted_iota(jnp.int32, rows.shape, 1)
    zero = jnp.zeros_like(rows)
    return jnp.concatenate([jnp.where((lane >= at) & (lane < at + HD), rows, zero) for at in lanes], 0)


def unstack(stacked, lanes):
    rows = stacked.shape[0] // 3
    lane = lax.broadcasted_iota(jnp.int32, (rows, stacked.shape[1]), 1)
    out = jnp.zeros((rows, stacked.shape[1]), stacked.dtype)
    for h, at in enumerate(lanes):
        out = jnp.where((lane >= at) & (lane < at + HD), stacked[h * rows : (h + 1) * rows], out)
    return out


def thirds(column):
    rows = column.shape[0] // 3
    return [column[h * rows : (h + 1) * rows] for h in range(3)]


def half(tile, upper):
    lane = lax.broadcasted_iota(jnp.int32, tile.shape, 1)
    return jnp.where((lane >= HD) if upper else (lane < HD), tile, jnp.zeros_like(tile))


def lanes_of(columns, rows):
    lane = lax.broadcasted_iota(jnp.int32, (rows, 2 * HD), 1)
    out = jnp.zeros((rows, 2 * HD), F32)
    for at, column in enumerate(columns):
        out = jnp.where(lane == at, column, out)
    return out


def hi_lo(value):
    hi = value.astype(BF16).astype(F32)
    return hi, value - hi


def norm_rows(hidden):
    center = hidden - jnp.mean(hidden, -1, keepdims=True)
    inverse = lax.rsqrt(jnp.mean(center * center, -1, keepdims=True) + EPS)
    return center * inverse, inverse


def norm_rows_back(grad, normed, inverse, gain):
    scaled = grad * gain
    return inverse * (
        scaled
        - jnp.mean(scaled, -1, keepdims=True)
        - normed * jnp.mean(scaled * normed, -1, keepdims=True)
    )


def project_kernel(x_ref, gain_ref, shift_ref, raw_ref, first_ref, q_ref, kv_ref, w_ref):
    @pl.when(pl.program_id(0) == 0)
    def _():
        scale = jnp.asarray(1.0 / math.sqrt(HD), BF16)
        blank = jnp.zeros((w_ref.shape[0], HD), BF16)
        w_ref[:, : 2 * HD] = jnp.concatenate([raw_ref[0, :, 2 * HD :] * scale, blank], 1)
        w_ref[:, 2 * HD : 4 * HD] = raw_ref[0, :, : 2 * HD] * scale
        w_ref[:, 4 * HD : 6 * HD] = raw_ref[2, :, : 2 * HD]
        w_ref[:, 6 * HD : 8 * HD] = jnp.concatenate([raw_ref[1, :, 2 * HD :], raw_ref[2, :, 2 * HD :]], 1)
        w_ref[:, 8 * HD :] = raw_ref[1, :, : 2 * HD]

    normed, _ = norm_rows(x_ref[...].astype(F32))
    first = (normed * gain_ref[...][None] + shift_ref[...][None]).astype(BF16)
    first_ref[...] = first
    out = dot_nn(first, w_ref[...]).astype(BF16)
    q_ref[...] = out[:, : 4 * HD]
    kv_ref[...] = out[:, 4 * HD :]


def project(x, gain, shift, raw):
    rows, width = x.shape
    tile = min(rows, 256)
    row = lambda w: pl.BlockSpec((tile, w), lambda i: (i, 0))
    vector = pl.BlockSpec((width,), lambda i: (0,))
    whole = lambda w: pl.BlockSpec((width, w), lambda i: (0, 0))
    low = lambda *shape: sds(shape, BF16)
    return pl.pallas_call(
        project_kernel,
        grid=(rows // tile,),
        out_shape=(low(rows, width), low(rows, 4 * HD), low(rows, 6 * HD), low(width, 10 * HD)),
        in_specs=[
            row(width), vector, vector, pl.BlockSpec(raw.shape, lambda i: (0, 0, 0)),
        ],
        out_specs=(row(width), row(4 * HD), row(6 * HD), whole(10 * HD)),
        compiler_params=PARAMS,
        cost_estimate=cost("project"),
        name="project",
    )(x, gain, shift, raw)


def dispatch_kernel(bd, index_ref, kv_ref, sent_ref, low_ref, high_ref):
    def step(slot, _):
        sent_ref[slot] = kv_ref[index_ref[slot]]
        return 0

    lax.fori_loop(0, sent_ref.shape[0], step, 0, unroll=4)
    for m in range(low_ref.shape[0]):
        low_ref[m] = kv_ref[m * bd]
        high_ref[m] = kv_ref[m * bd + bd - 1]


def bias_kernel(bd, blocks_all, table_ref, meta_ref, keep_ref, raw_ref, bias_ref, seq_ref, column_ref, wo_ref):
    wo_ref[:, : 2 * HD] = raw_ref[:, : 2 * HD]
    blank = jnp.zeros((wo_ref.shape[0], HD), BF16)
    wo_ref[:, 2 * HD :] = jnp.concatenate([blank, raw_ref[:, 2 * HD :]], 1)
    low = lambda keep: jnp.where(keep > 0, 0.0, NEG)
    for m in range(seq_ref.shape[0]):
        for b in range(bd):
            i = m * bd + b
            here = meta_ref[4] * bd + b

            def row(block, inside=True):
                return low(jnp.where(inside, keep_ref[pl.ds(m * blocks_all + block, 1)], 0))

            own = row(here)
            listed = [
                row(jnp.maximum(here - 1, 0), here > 0),
                own,
                row(jnp.minimum(here + 1, blocks_all - 1), here < blocks_all - 1),
                row(0),
                row(blocks_all - 1),
            ] + [row(table_ref[i * RANDS + j]) for j in range(RANDS)]
            bias_ref[i] = jnp.concatenate(listed, 1)
            seq_ref[m, :, b * BLOCK : (b + 1) * BLOCK] = own
            column_ref[i] = jnp.transpose(jnp.broadcast_to(own, (4 * HD, BLOCK)))


def gather_kernel(index_ref, blocks_ref, out_ref):
    def step(slot, _):
        out_ref[slot] = blocks_ref[index_ref[slot]]
        return 0

    lax.fori_loop(0, out_ref.shape[0], step, 0, unroll=4)


def lead_fwd_kernel(
    meta_ref, kv_ref, bias_ref, x0_ref, x1_ref, gain_ref, shift_ref, w_ref, first0_ref, first1_ref,
    lead0_ref, lead1_ref, mine_ref, given_ref,
):
    for x_ref, first_ref, lead_ref in ((x0_ref, first0_ref, lead0_ref), (x1_ref, first1_ref, lead1_ref)):
        normed, _ = norm_rows(x_ref[...].reshape(-1, x_ref.shape[2]).astype(F32))
        first = (normed * gain_ref[...][None] + shift_ref[...][None]).astype(BF16)
        first_ref[...] = first
        lead_ref[...] = dot_nn(first, w_ref[...]).astype(BF16).reshape(lead_ref.shape)
    low = meta_ref[3]
    for m in range(kv_ref.shape[0]):
        queries = jnp.concatenate([lead0_ref[m, :, : 4 * HD], lead1_ref[m, :, : 4 * HD]], 0)
        scores = dot_nt(stack(queries, Q_LANES), kv_ref[m, :, K_PART]) + bias_ref[m]
        top = jnp.max(scores, -1, keepdims=True)
        expo = jnp.exp(scores - top)
        total = jnp.sum(expo, -1, keepdims=True)
        out = unstack(dot_nn(expo.astype(BF16), kv_ref[m, :, V_PART]), O_LANES)
        stats = lanes_of(thirds(top) + thirds(total), 2 * BLOCK)
        for part_ref, first in ((mine_ref, low == 1), (given_ref, low == 0)):
            for lanes, value in ((slice(0, 2 * HD), out[:, : 2 * HD]), (slice(2 * HD, 4 * HD), out[:, 2 * HD :] + stats)):
                part_ref[m, :, lanes] = jnp.where(first, value[:BLOCK], value[BLOCK:])


def merge_parts(parts):
    lane = lax.broadcasted_iota(jnp.int32, (BLOCK, 2 * HD), 1)
    stats = [p[:, 2 * HD :] for p in parts]
    top = stats[0]
    for st in stats[1:]:
        top = jnp.maximum(top, st)
    tops = [top[:, h : h + 1] for h in range(3)]
    sums = [0.0, 0.0, 0.0]
    out0, out1 = 0.0, 0.0
    for p, st in zip(parts, stats):
        scale = [jnp.exp(st[:, h : h + 1] - tops[h]) for h in range(3)]
        sums = [sums[h] + st[:, 3 + h : 4 + h] * scale[h] for h in range(3)]
        out0 = out0 + p[:, : 2 * HD] * jnp.where(lane < HD, scale[0], scale[1])
        out1 = out1 + st * scale[2]
    return out0, jnp.where(lane >= HD, out1, 0.0), tops, sums


def merge_kernel(a_ref, b_ref, out_ref):
    for m in range(a_ref.shape[0]):
        out0, out1, tops, sums = merge_parts([a_ref[m], b_ref[m]])
        out_ref[m, :, : 2 * HD] = out0
        out_ref[m, :, 2 * HD :] = out1 + lanes_of(tops + sums, BLOCK)


def merge(a, b):
    return call(merge_kernel, sds(a.shape, F32), name="merge", limit=SMALL)(a, b)


def lead_finish_kernel(*refs):
    part_refs, (out_ref, lse_ref) = refs[:-2], refs[-2:]
    lane = lax.broadcasted_iota(jnp.int32, (BLOCK, 2 * HD), 1)
    for m in range(out_ref.shape[0]):
        out0, out1, tops, sums = merge_parts([p[m] for p in part_refs])
        out_ref[m, :, : 2 * HD] = (out0 / jnp.where(lane < HD, sums[0], sums[1])).astype(BF16)
        out_ref[m, :, 2 * HD :] = (out1 / sums[2]).astype(BF16)
        lse_ref[m] = lanes_of([tops[h] + jnp.log(sums[h]) for h in range(3)], BLOCK)


def fill_ext(ext_ref, kv_ref, low_ref, high_ref, seqs, per):
    for m in range(seqs):
        ext_ref[m, :BLOCK] = low_ref[m]
        ext_ref[m, BLOCK : BLOCK + per] = kv_ref[m]
        ext_ref[m, BLOCK + per :] = high_ref[m]


def fill_listed(listed_ref, ext_ref, lead0_ref, lead1_ref, rand_ref, slot_ref, m, b, block):
    listed_ref[: 3 * BLOCK] = ext_ref[m, pl.ds(pl.multiple_of(b * BLOCK, BLOCK), 3 * BLOCK)]
    listed_ref[3 * BLOCK : 4 * BLOCK] = lead0_ref[m, :, 4 * HD :]
    listed_ref[4 * BLOCK : 5 * BLOCK] = lead1_ref[m, :, 4 * HD :]
    for j in range(RANDS):
        listed_ref[(5 + j) * BLOCK : (6 + j) * BLOCK] = rand_ref[slot_ref[block * RANDS + j]]


def pos_of(meta_ref, at):
    j = at ^ meta_ref[0]
    return ((j & 1) << 1) | (j >> 1)


def sparse_fwd_kernel(
    first, seqs, per, share, slot_ref, meta_ref, q_ref, kv_ref, low_ref, high_ref, lead0_ref,
    lead1_ref, rand_ref, bias_ref, out_ref, lse_ref, ext_ref, listed_ref,
):
    blocks = per // BLOCK
    chunk = min(share, BLOCK)
    fill_ext(ext_ref, kv_ref, low_ref, high_ref, seqs, per)

    def attend(i, here):
        m, b = i // blocks, i % blocks
        fill_listed(here, ext_ref, lead0_ref, lead1_ref, rand_ref, slot_ref, m, b, first + i)
        scores = dot_nt(stack(q_ref[i], Q_LANES), here[:, K_PART]) + bias_ref[i]
        top = jnp.max(scores, -1, keepdims=True)
        expo = jnp.exp(scores - top)
        total = jnp.sum(expo, -1, keepdims=True)
        prob = (expo * (1.0 / total)).astype(BF16)
        out = unstack(dot_nn(prob, here[:, V_PART]), O_LANES).astype(BF16)
        lse_ref[pl.ds(pl.multiple_of(i * BLOCK, BLOCK), BLOCK)] = lanes_of(
            thirds(top + jnp.log(total)), BLOCK
        )
        for c in range(BLOCK // chunk):
            token = b * BLOCK + c * chunk
            at = token // share
            row = pos_of(meta_ref, at) * (seqs * share) + m * share + (token - at * share)
            rows = pl.ds(pl.multiple_of(row, chunk), chunk)
            out_ref[rows] = out[c * chunk : (c + 1) * chunk]

    def step(j, _):
        attend(2 * j, listed_ref.at[0])
        attend(2 * j + 1, listed_ref.at[1])
        return 0

    lax.fori_loop(0, seqs * blocks // 2, step, 0)


def out_project_kernel(groups, seqs, per, share, meta_ref, wo_ref, lead_out_ref, *refs):
    attn_refs, mixed_refs, part_refs = refs[:groups], refs[groups : 2 * groups], refs[2 * groups :]
    blocks = per // BLOCK
    chunk = min(share, BLOCK)
    piece = seqs * share
    for g in range(groups):
        mixed_refs[g][...] = attn_refs[g][...]
    for end, b in ((1, 0), (2, blocks - 1)):

        @pl.when(meta_ref[end] == 1)
        def _(b=b):
            for g in range(groups):
                for m in range(seqs):
                    for c in range(BLOCK // chunk):
                        token = b * BLOCK + c * chunk
                        at = token // share
                        row = pos_of(meta_ref, at) * piece + m * share + (token - at * share)
                        rows = pl.ds(pl.multiple_of(row, chunk), chunk)
                        mixed_refs[g][rows] = lead_out_ref[g * seqs + m, c * chunk : (c + 1) * chunk]

    wo = wo_ref[...]
    for g in range(groups):
        for k in range(4):
            rows = slice(k * piece, (k + 1) * piece)
            part_refs[4 * g + k][...] = dot_nt(mixed_refs[g][rows], wo).astype(BF16)


def down_kernel(groups, *refs):
    up_refs, w_ref, out_refs = refs[: 4 * groups], refs[4 * groups], refs[4 * groups + 1 :]
    rows = up_refs[0].shape[0]
    for g in range(groups):
        for k in range(4):
            out = dot_nt(up_refs[4 * g + k][...], w_ref[...]).astype(BF16)
            out_refs[k][g * rows : (g + 1) * rows] = out


def total_of(refs):
    return refs[0][...].astype(F32) + refs[1][...].astype(F32) + refs[2][...].astype(F32)


def mid_fwd_kernel(meta_ref, x_ref, own_ref, core_ref, y_ref, gain_ref, shift_ref, hidden_ref, act_ref):
    x = x_ref[...].reshape(hidden_ref.shape).astype(F32)
    hidden = total_of((own_ref, core_ref, y_ref)) + x
    normed, _ = norm_rows(hidden)
    hidden_ref[...] = hidden
    act_ref[...] = (normed * gain_ref[...][None] + shift_ref[...][None]).astype(BF16)


def ffn_kernel(meta_ref, *refs):
    gu_refs, act_refs, w_ref, outs = refs[:4], refs[4:8], refs[8], refs[9:]
    rows = act_refs[0].shape[0]
    for k in (3, 2, 1, 0):
        up_ref, pre_ref, back_ref = outs[3 * k : 3 * k + 3]
        pre = dot_nn(act_refs[k][...], w_ref[...])
        phi = 0.5 + 0.5 * lax.erf(pre * (1.0 / math.sqrt(2.0)))
        density = jnp.exp(-0.5 * pre * pre) * (1.0 / math.sqrt(2.0 * math.pi))
        up_ref[...] = (pre * phi).astype(BF16)
        gu = gu_refs[k][...].reshape(rows, gu_refs[k].shape[2])
        grad_pre = (gu * (phi + pre * density)).astype(BF16)
        pre_ref[...] = grad_pre
        back_ref[...] = dot_nt(grad_pre, w_ref[...]).astype(BF16)


def mid_bwd_kernel(
    meta_ref, og_ref, own_ref, core_ref, y_ref, hidden_ref, gain_ref, total_ref, low_ref, sums_ref
):
    grad = total_of((own_ref, core_ref, y_ref))
    normed, inverse = norm_rows(hidden_ref[...])
    og = og_ref[...].reshape(hidden_ref.shape).astype(F32)
    total = og + norm_rows_back(grad, normed, inverse, gain_ref[...][None])
    total_ref[...] = total
    low_ref[...] = total.astype(BF16)
    sums_ref[0:1] = jnp.sum(grad * normed, 0, keepdims=True)
    sums_ref[1:2] = jnp.sum(grad, 0, keepdims=True)


def end_kernel(groups, meta_ref, *refs):
    x_refs, refs = refs[:groups], refs[groups:]
    own_ref, core_ref, y_ref = refs[:3]
    gain_ref, out_ref = refs[-2:]
    seqs = x_refs[0].shape[0]
    rows = own_ref.shape[0] // groups
    for g in range(groups):
        part = slice(g * rows, (g + 1) * rows)
        grad = total_of([ref.at[part] for ref in (own_ref, core_ref, y_ref)])
        normed, inverse = norm_rows(x_refs[g][...].reshape(grad.shape).astype(F32))
        total = refs[3 + g][...] + norm_rows_back(grad, normed, inverse, gain_ref[...][None])
        out_ref[g * seqs : (g + 1) * seqs] = total.reshape(x_refs[g].shape)


def output_kernel(groups, own_ref, core_ref, y_ref, *refs):
    out_ref = refs[-1]
    seqs, share, width = out_ref.shape
    seqs //= groups
    rows = seqs * share
    for g in range(groups):
        part = slice(g * rows, (g + 1) * rows)
        total = total_of([ref.at[part] for ref in (own_ref, core_ref, y_ref)]) + refs[g][...]
        out_ref[g * seqs : (g + 1) * seqs] = total.reshape(seqs, share, width)


def lead_grad_kernel(groups, seqs, per, share, meta_ref, wo_ref, lead_lse_ref, lead_out_ref, *refs):
    pieces, lead_ref, rows_ref = refs[:-2], refs[-2], refs[-1]
    blocks = per // BLOCK
    chunk = min(share, BLOCK)
    root = (meta_ref[1] + meta_ref[2]) == 1
    lead_ref[...] = jnp.zeros_like(lead_ref)
    token = jnp.where(meta_ref[1] == 1, 0, (blocks - 1) * BLOCK)
    for g in range(groups):
        for m in range(seqs):
            for c in range(BLOCK // chunk):
                at = (token + c * chunk) // share
                inside = pl.multiple_of(m * share + (token + c * chunk - at * share), chunk)
                for k in range(4):

                    @pl.when(root & (pos_of(meta_ref, at) == k))
                    def _(k=k, g=g, m=m, c=c, inside=inside):
                        to = (g * seqs + m) * BLOCK + c * chunk
                        rows_ref[to : to + chunk] = pieces[4 * g + k][pl.ds(inside, chunk)]

    @pl.when(root)
    def _():
        total = groups * seqs * BLOCK
        grad = dot_nn(rows_ref[...], wo_ref[...])
        low = grad.astype(BF16)
        prod = low.astype(F32) * lead_out_ref[...].reshape(total, 4 * HD).astype(F32)
        deltas = [
            jnp.sum(half(prod[:, : 2 * HD], False), -1, keepdims=True),
            jnp.sum(half(prod[:, : 2 * HD], True), -1, keepdims=True),
            jnp.sum(half(prod[:, 2 * HD :], True), -1, keepdims=True),
        ]
        d_hi, d_lo = zip(*(hi_lo(d) for d in deltas))
        lse = lead_lse_ref[...].reshape(total, 2 * HD)
        l_hi, l_lo = zip(*(hi_lo(lse[:, h : h + 1]) for h in range(3)))
        stats = lanes_of(l_hi + l_lo + d_hi + d_lo, total)
        tile1 = (half(grad[:, 2 * HD :], True) + stats).astype(BF16)
        lead_ref[:, :, : 2 * HD] = low[:, : 2 * HD].reshape(groups * seqs, BLOCK, 2 * HD)
        lead_ref[:, :, 2 * HD :] = tile1.reshape(groups * seqs, BLOCK, 2 * HD)


def heads_grad_kernel(groups, seqs, per, share, index_ref, meta_ref, wo_ref, *refs):
    pieces, mixed_refs = refs[: 4 * groups], refs[4 * groups : 5 * groups]
    lse_refs = refs[5 * groups : 6 * groups]
    grads_ref, sent_ref = refs[6 * groups :]
    wo = wo_ref[...]
    blocks = per // BLOCK
    rows_of = seqs * share
    for g in range(groups):
        for k in range(4):
            grad = dot_nn(pieces[4 * g + k][...], wo)
            low = grad.astype(BF16)
            prod = low.astype(F32) * mixed_refs[g][k * rows_of : (k + 1) * rows_of].astype(F32)
            deltas = [
                jnp.sum(half(prod[:, : 2 * HD], False), -1, keepdims=True),
                jnp.sum(half(prod[:, : 2 * HD], True), -1, keepdims=True),
                jnp.sum(half(prod[:, 2 * HD :], True), -1, keepdims=True),
            ]
            d_hi, d_lo = zip(*(hi_lo(d) for d in deltas))
            spare = [jnp.zeros_like(d_hi[0])] * 6
            stats = lanes_of(spare + list(d_hi + d_lo), rows_of)
            for m in range(seqs):
                at = slice(m * share, (m + 1) * share)
                inside = m * per + (meta_ref[0] ^ SWAP[k]) * share
                rows = pl.ds(pl.multiple_of(g * seqs * per + inside, share), share)
                lse = lse_refs[g][pl.ds(pl.multiple_of(inside, share), share)]
                l_hi, l_lo = zip(*(hi_lo(lse[:, h : h + 1]) for h in range(3)))
                grads_ref[rows, : 2 * HD] = low[at, : 2 * HD]
                grads_ref[rows, 2 * HD :] = (
                    half(grad[at, 2 * HD :], True) + stats[at] + lanes_of(l_hi + l_lo, share)
                ).astype(BF16)
    lane = lax.broadcasted_iota(jnp.int32, (BLOCK, 2 * HD), 1)
    for end, b in ((1, 0), (2, blocks - 1)):

        @pl.when(meta_ref[end] == 1)
        def _(b=b):
            for m in range(groups * seqs):
                rows = slice(m * per + b * BLOCK, m * per + (b + 1) * BLOCK)
                tile1 = grads_ref[rows, 2 * HD :].astype(F32)
                grads_ref[rows, : 2 * HD] = jnp.zeros((BLOCK, 2 * HD), BF16)
                grads_ref[rows, 2 * HD :] = jnp.where(lane < 6, tile1, 0.0).astype(BF16)

    def send(slot, _):
        at = pl.multiple_of(index_ref[slot] * BLOCK, BLOCK)
        sent_ref[slot] = grads_ref[pl.ds(at, BLOCK)]
        return 0

    lax.fori_loop(0, sent_ref.shape[0], send, 0, unroll=4)


def row_stats(tile):
    st = tile.astype(F32)
    lse = [st[:, h : h + 1] + st[:, 3 + h : 4 + h] for h in range(3)]
    delta = [st[:, 6 + h : 7 + h] + st[:, 9 + h : 10 + h] for h in range(3)]
    return lse, delta


def kv_grad(v_part, k_part):
    return jnp.concatenate([v_part[:, : 2 * HD], v_part[:, 2 * HD :] + k_part[:, : 2 * HD], k_part[:, 2 * HD :]], 1)


def sparse_bwd_kernel(
    batches, per, slot_ref, q_ref, kv_ref, low_ref, high_ref, lead0_ref, lead1_ref, rand_ref,
    bias_ref, grads_ref, dq_ref, dkv_ref, ret_low_ref, ret_high_ref, dlead0_ref, dlead1_ref,
    ext_ref, listed_ref, dext_ref, dlead_ref,
):
    blocks = per // BLOCK
    near = 6 * BLOCK
    fill_ext(ext_ref, kv_ref, low_ref, high_ref, batches, per)
    dext_ref[...] = jnp.zeros_like(dext_ref)
    dlead_ref[...] = jnp.zeros_like(dlead_ref)

    def attend(i, here):
        m, b = i // blocks, i % blocks
        fill_listed(here, ext_ref, lead0_ref, lead1_ref, rand_ref, slot_ref, m, b, i)
        grads = grads_ref[i]
        lse, delta = row_stats(grads[:, 2 * HD :])
        queries, grads = stack(q_ref[i], Q_LANES), stack(grads, O_LANES)
        prob = jnp.exp(dot_nt(queries, here[:, K_PART]) + bias_ref[i] - jnp.concatenate(lse, 0))
        ds = prob * (dot_nt(grads, here[:, V_PART]) - jnp.concatenate(delta, 0))
        ds = ds.astype(BF16)
        dq_ref[i] = unstack(dot_nn(ds, here[:, K_PART]), Q_LANES)
        dkv = kv_grad(dot_tn(prob[:, :near].astype(BF16), grads), dot_tn(ds[:, :near], queries))
        return m, b, dkv

    def step(j, _):
        done = [attend(2 * j + n, listed_ref.at[n]) for n in range(2)]
        for m, b, dkv in done:
            dext_ref[m, pl.ds(pl.multiple_of(b * BLOCK, BLOCK), 3 * BLOCK)] += dkv[: 3 * BLOCK]
            dlead_ref[m] += dkv[3 * BLOCK : 5 * BLOCK]
        return 0

    lax.fori_loop(0, batches * blocks // 2, step, 0)
    for m in range(batches):
        ret_low_ref[m] = dext_ref[m, :BLOCK].astype(BF16)
        dkv_ref[m] = dext_ref[m, BLOCK : BLOCK + per]
        ret_high_ref[m] = dext_ref[m, BLOCK + per :].astype(BF16)
        dlead0_ref[m] = dlead_ref[m, :BLOCK]
        dlead1_ref[m] = dlead_ref[m, BLOCK:]


def lead_bwd_kernel(
    meta_ref, lead0_ref, lead1_ref, kv_ref, bias_ref, sparse_ref, dlead0_ref, dlead1_ref, do0_ref, do1_ref,
    dkv_ref, mine_ref, given_ref,
):
    low = meta_ref[3]
    for m in range(kv_ref.shape[0]):
        grads = jnp.concatenate([do0_ref[m], do1_ref[m]], 0)
        lse, delta = row_stats(grads[:, 2 * HD :])
        queries = jnp.concatenate([lead0_ref[m, :, : 4 * HD], lead1_ref[m, :, : 4 * HD]], 0)
        queries, grads = stack(queries, Q_LANES), stack(grads, O_LANES)
        keys, values = kv_ref[m, :, K_PART], kv_ref[m, :, V_PART]
        prob = jnp.exp(dot_nt(queries, keys) + bias_ref[m] - jnp.concatenate(lse, 0))
        ds = (prob * (dot_nt(grads, values) - jnp.concatenate(delta, 0))).astype(BF16)
        dq = unstack(dot_nn(ds, keys), Q_LANES)
        for part_ref, first in ((mine_ref, low == 1), (given_ref, low == 0)):
            part_ref[m, :, : 4 * HD] = jnp.where(first, dq[:BLOCK], dq[BLOCK:]).astype(BF16)
            part_ref[m, :, 4 * HD :] = jnp.where(first, dlead0_ref[m], dlead1_ref[m]).astype(BF16)
        dkv_ref[m] = sparse_ref[m] + kv_grad(dot_tn(prob.astype(BF16), grads), dot_tn(ds, queries))


def split_rows(meta_ref, grad_ref, keep_ref, send_ref, lanes=slice(None)):
    count, rows, _ = keep_ref.shape
    even = (meta_ref[4] & 1) == 0
    for z in range(count):
        one = grad_ref[2 * z * rows : (2 * z + 1) * rows, lanes].astype(BF16)
        two = grad_ref[(2 * z + 1) * rows : (2 * z + 2) * rows, lanes].astype(BF16)
        keep_ref[z] = jnp.where(even, one, two)
        send_ref[z] = jnp.where(even, two, one)


def ffn_grad_kernel(groups, seqs, per, share, meta_ref, og_ref, *refs):
    count = 4 * groups
    ups, acts, pres = (refs[n * count : (n + 1) * count] for n in range(3))
    keep0_ref, send0_ref, keep1_ref, send1_ref, left_ref, right_ref, grad_ref = refs[3 * count :]
    piece = seqs * share
    hidden = ups[0].shape[1]
    for g in range(groups):
        for k in range(4):
            for m in range(seqs):
                row = (g * seqs + m) * per + (meta_ref[0] ^ SWAP[k]) * share
                rows = pl.ds(pl.multiple_of(row, share), share)
                right_ref[rows] = ups[4 * g + k][m * share : (m + 1) * share]
    grad_ref[:, :hidden] = dot_tn(og_ref[...], right_ref[...])
    for n in range(count):
        left_ref[n * piece : (n + 1) * piece] = acts[n][...]
        right_ref[n * piece : (n + 1) * piece] = pres[n][...]
    grad_ref[:, hidden:] = dot_tn(left_ref[...], right_ref[...])
    split_rows(meta_ref, grad_ref, keep0_ref, send0_ref, slice(0, hidden))
    split_rows(meta_ref, grad_ref, keep1_ref, send1_ref, slice(hidden, 2 * hidden))


def fold_kernel(count, meta_ref, *refs):
    pairs, out_refs = refs[: 2 * count], refs[2 * count :]
    z = meta_ref[4] >> 1
    for n, ref in enumerate(out_refs):
        at = 0
        for keep_ref, got_ref in zip(pairs[::2], pairs[1::2]):
            lanes = keep_ref.shape[2]
            total = keep_ref[z ^ n].astype(F32) + got_ref[z ^ n].astype(F32)
            ref[:, at : at + lanes] = total.astype(ref.dtype)
            at += lanes


def slots_kernel(
    index_ref, valid_ref, q_got_ref, do_got_ref, kv_ref, column_ref, dkv_ref, acc_ref
):
    acc_ref[...] = dkv_ref[...]

    def block_grads(c):
        at = index_ref[c]
        live = valid_ref[c] == 1
        kv = kv_ref[at]
        grads = do_got_ref[c]
        stats = jnp.transpose(grads[:, 2 * HD :].astype(F32))
        lse = [stats[h : h + 1] + stats[3 + h : 4 + h] for h in range(3)]
        delta = [stats[6 + h : 7 + h] + stats[9 + h : 10 + h] for h in range(3)]
        queries, grads = stack(q_got_ref[c], Q_LANES), stack(grads, O_LANES)
        bias = column_ref[at][:, : 3 * BLOCK]
        prob = jnp.exp(dot_nt(kv[:, K_PART], queries) + bias - jnp.concatenate(lse, 1))
        prob = jnp.where(live, prob, 0.0)
        ds = prob * (dot_nt(kv[:, V_PART], grads) - jnp.concatenate(delta, 1))
        return at, kv_grad(dot_nn(prob.astype(BF16), grads), dot_nn(ds.astype(BF16), queries))

    slots = q_got_ref.shape[0]
    wide = 4 if slots % 4 == 0 else 1

    def slot(j, _):
        done = [block_grads(wide * j + n) for n in range(wide)]
        for at, grad in done:
            acc_ref[at] += grad
        return 0

    lax.fori_loop(0, slots // wide, slot, 0)


def tail_kernel(
    groups, seqs, per, share, devices, meta_ref, dq_ref, dkv_ref, ret_low_ref, ret_high_ref, first_ref, first0_ref,
    first1_ref, mine_ref, given_ref, *refs,
):
    pieces, mixed_refs = refs[: 4 * groups], refs[4 * groups : 5 * groups]
    w_ref, gain_ref, shift_ref = refs[5 * groups : 5 * groups + 3]
    count = 4
    sums_refs = refs[5 * groups + 3 : 6 * groups + 3]
    ends_refs, back_refs = refs[6 * groups + 3 : -count - 5], refs[-count - 5 : -5]
    keep_ref, send_ref, gqkv_ref, grad_ref, left_ref = refs[-5:]
    blocks = per // BLOCK
    batches = dkv_ref.shape[0] // blocks
    gqkv_ref[:, : 4 * HD] = dq_ref[...].reshape(-1, 4 * HD).astype(BF16)
    gqkv_ref[:, 4 * HD :] = dkv_ref[...].reshape(-1, 6 * HD).astype(BF16)
    for m in range(batches):
        i = m * blocks
        low, high = ret_low_ref[m].astype(F32), ret_high_ref[m].astype(F32)
        if blocks == 1:
            gqkv_ref[i * BLOCK : (i + 1) * BLOCK, 4 * HD :] = (dkv_ref[i] + low + high).astype(BF16)
        else:
            j = i + blocks - 1
            gqkv_ref[i * BLOCK : (i + 1) * BLOCK, 4 * HD :] = (dkv_ref[i] + low).astype(BF16)
            gqkv_ref[j * BLOCK : (j + 1) * BLOCK, 4 * HD :] = (dkv_ref[j] + high).astype(BF16)
    lead = meta_ref[3] == 1
    rows = batches * BLOCK
    mine, given = mine_ref[...].reshape(rows, 10 * HD), given_ref[...].reshape(rows, 10 * HD)
    ends = jnp.concatenate([jnp.where(lead, mine, given), jnp.where(lead, given, mine)], 0)
    firsts = jnp.concatenate([first0_ref[...], first1_ref[...]], 0)
    grad = dot_tn(first_ref[...], gqkv_ref[...]) + dot_tn(firsts, ends)
    grad_ref[:, : 10 * HD] = grad
    columns = jnp.sum(gqkv_ref[...].astype(F32), 0, keepdims=True)
    columns = columns + jnp.sum(ends.astype(F32), 0, keepdims=True)
    weights = w_ref[...].astype(F32)
    along = jnp.sum(grad * weights, -1, keepdims=True)
    shift_sum = jnp.sum(columns * weights, -1, keepdims=True)
    rows_in = [gain_ref[...][None], shift_ref[...][None]]
    rows_in += [sum(ref[n : n + 1] for ref in sums_refs) for n in range(2)]
    rows_in.append(jnp.zeros((4, grad.shape[0]), F32))
    gain, shift, gain2_sum, shift2_sum = (
        jnp.transpose(jnp.concatenate(rows_in, 0))[:, n : n + 1] for n in range(4)
    )
    stats = lanes_of([(along - shift * shift_sum) / gain, shift_sum, gain2_sum, shift2_sum], grad.shape[0])
    lane = lax.broadcasted_iota(jnp.int32, stats.shape, 1)
    moved = jnp.concatenate([stats[:, HD:], stats[:, :HD]], 1)
    grad_ref[:, : 2 * HD] = jnp.where(lane < HD, grad[:, : 2 * HD], moved)
    piece = pieces[0].shape[0]
    total = 0.0
    for g in range(groups):
        for k in range(4):
            left_ref[k * piece : (k + 1) * piece] = pieces[4 * g + k][...]
        total = total + dot_tn(left_ref[...], mixed_refs[g][...])
    grad_ref[:, 10 * HD :] = total
    split_rows(meta_ref, grad_ref, keep_ref, send_ref)
    for end, b in ((1, 0), (2, blocks - 1)):

        @pl.when(meta_ref[end] == 1)
        def _(b=b):
            for m in range(groups * seqs):
                rows = slice(m * per + b * BLOCK, m * per + (b + 1) * BLOCK)
                total = gqkv_ref[rows].astype(F32)
                for ref in ends_refs:
                    total = total + ref[m].astype(F32)
                gqkv_ref[rows] = total.astype(BF16)

    for g in range(groups):
        for k in range(4):
            for m in range(seqs):
                row = (g * seqs + m) * per + (meta_ref[0] ^ SWAP[k]) * share
                rows = pl.ds(pl.multiple_of(row, share), share)
                back = dot_nt(gqkv_ref[rows], w_ref[...]).astype(BF16)
                back_refs[k][(g * seqs + m) * share : (g * seqs + m + 1) * share] = back


def swap_tp(value, bit):
    return lax.ppermute(value, "tp", [(i, i ^ bit) for i in range(lax.axis_size("tp"))])


def scatter_tp(parts):
    far = swap_tp(parts[3], 1)
    near = swap_tp(parts[2], 1)
    both = (parts[1].astype(F32) + far.astype(F32)).astype(BF16)
    return parts[0], near, swap_tp(both, 2)


def gather_tp(piece, before_first=(), before_last=()):
    cross = swap_tp(after(piece, *before_first) if before_first else piece, 2)
    return piece, cross, swap_tp(piece, 1), swap_tp(after(cross, *before_last) if before_last else cross, 1)


def mirrored(pairs, last):
    return pairs + [(last - a, last - b) for a, b in pairs]


SECOND = [(1, 3), (4, 5), (2, 6), (0, 7)]


def in_first_group(myself, devices):
    if devices == 8:
        return (myself == 0) | (myself == 1) | (myself == 2) | (myself == 4)
    return myself < devices // 2


def spread(own, myself, devices, *before_last):
    last = devices - 1
    held = own
    if devices == 8:
        for k in (1, 2, 4):
            held = held + lax.ppermute(own, "seq", mirrored([(0, k)], last))
        held = after(held, *before_last)
        other = lax.ppermute(held, "seq", mirrored(SECOND, last))
    else:
        bit = 1
        while bit < devices // 2:
            held = held + lax.ppermute(held, "seq", mirrored([(i, i + bit) for i in range(bit)], last))
            bit *= 2
        other = lax.ppermute(held, "seq", [(i, i ^ bit) for i in range(devices)])
    first = in_first_group(myself, devices)
    return jnp.where(first, held, other), jnp.where(first, other, held), other


def collect_first(given, devices):
    last = devices - 1
    if devices == 8:
        return lax.ppermute(given, "seq", mirrored([(b, a) for a, b in SECOND], last))
    return lax.ppermute(given, "seq", [(i, i ^ (devices // 2)) for i in range(devices)])


def collect_rest(mine, devices, join):
    last = devices - 1
    if devices == 8:
        return [mine] + [lax.ppermute(mine, "seq", mirrored([(k, 0)], last)) for k in (1, 2, 4)]
    bit = devices // 2
    while bit > 1:
        bit //= 2
        mine = join(mine, lax.ppermute(mine, "seq", mirrored([(i + bit, i) for i in range(bit)], last)))
    return [mine]


def to_owners(slots):
    return lax.all_to_all(slots, "seq", split_axis=0, concat_axis=0, tiled=True)


def sum_seq_first(send, devices):
    return lax.ppermute(send, "seq", [(i, i ^ 1) for i in range(devices)])


def sum_seq_rest(pairs, meta, devices):
    count, rows = pairs[0][0].shape[:2]
    lanes = sum(keep.shape[2] for keep, _ in pairs)
    if count == 4:
        low = sds((rows, lanes), BF16)
        own, *out = call(
            partial(fold_kernel, len(pairs)), (sds((rows, lanes), F32), low, low, low), name="fold"
        )(*(v for pair in pairs for v in pair), smem=(meta,))
        return [own] + [
            lax.ppermute(piece, "seq", [(i, i ^ (2 * (n + 1))) for i in range(devices)])
            for n, piece in enumerate(out)
        ]
    total = [(keep.astype(F32) + got.astype(F32)).astype(BF16) for keep, got in pairs]
    return across(jnp.concatenate(total, 2), devices)


def across(total, devices):
    sides = [[i for i in range(devices) if i % 2 == side] for side in range(2)]
    got = lax.all_to_all(
        total, "seq", split_axis=0, concat_axis=0, tiled=True, axis_index_groups=sides
    )
    return [got[n] for n in range(total.shape[0])]


def sum_of(terms):
    total = terms[0].astype(F32)
    for term in terms[1:]:
        total = total + term.astype(F32)
    return total


def per_device(
    layer_input,
    out_grad,
    norm1_gain,
    norm1_shift,
    w_qkv,
    w_out,
    norm2_gain,
    norm2_shift,
    w_up,
    w_down,
    key_keep,
    rand_blocks,
):
    batches, per, width = layer_input.shape
    local = w_qkv.shape[2]
    devices = lax.axis_size("seq")
    myself = lax.axis_index("seq")
    tp_count = lax.axis_size("tp")
    tp_place = lax.axis_index("tp")
    assert local == 3 * HD and tp_count == 4 and devices % 2 == 0 and batches % 2 == 0
    share = per // tp_count
    bd = per // BLOCK
    total = batches * bd
    blocks_all = bd * devices
    groups = 2
    seqs = batches // groups
    piece = seqs * share
    refs = total * RANDS
    slots_per = max(1, -(-refs // devices))
    slots = devices * slots_per
    hidden_here = w_up.shape[1]
    rows = width // devices
    i32 = jnp.int32
    flag = lambda v: v.astype(i32)
    meta = jnp.stack(
        [
            tp_place, flag(myself == 0), flag(myself == devices - 1), flag(in_first_group(myself, devices)), myself,
        ]
    ).astype(i32)

    CHAIN.last = ()
    scale = 1.0 / math.sqrt(HD)
    x_rows = layer_input.reshape(batches * per, width)
    first, q, kv, w640 = CHAIN.done(project(x_rows, norm1_gain, norm1_shift, w_qkv.transpose(1, 0, 2)))
    is_first, is_last = myself == 0, myself == devices - 1
    ends = jnp.where(is_first, layer_input[:, :BLOCK], layer_input[:, per - BLOCK :])
    ends = jnp.where(is_first | is_last, ends, jnp.zeros_like(ends))
    lead_x0, lead_x1, arrived = spread(ends, myself, devices, kv)
    q_blocks = q.reshape(total, BLOCK, 4 * HD)
    kv_blocks = kv.reshape(total, BLOCK, 6 * HD)
    kv_seqs = kv.reshape(batches, per, 6 * HD)

    table = (
        rand_blocks.reshape(batches, devices, bd, RANDS).transpose(1, 0, 2, 3).reshape(devices, refs)
    )
    owners = table // bd
    source = (jnp.arange(refs, dtype=i32) // (bd * RANDS))[None] * bd + table - owners * bd
    order = jnp.arange(refs, dtype=i32)
    earlier = order[None, :] < order[:, None]
    rank = jnp.sum(((owners[:, :, None] == owners[:, None, :]) & earlier[None]).astype(i32), -1)
    places = jnp.arange(slots_per, dtype=i32)
    asked = (owners == myself)[:, None, :] & (rank[:, None, :] == places[None, :, None])
    source_of = jnp.sum(jnp.where(asked, source[:, None, :], 0), -1).reshape(slots)
    valid = jnp.sum(asked.astype(i32), -1).reshape(slots)
    my_owner = lax.dynamic_index_in_dim(owners, myself, 0, False)
    my_rank = lax.dynamic_index_in_dim(rank, myself, 0, False)
    slot_of = my_owner * slots_per + my_rank
    mine = lax.dynamic_index_in_dim(table, myself, 0, False)
    query_of = jnp.sum(
        jnp.where(
            slot_of[None, :] == jnp.arange(slots, dtype=i32)[:, None], (order // RANDS)[None, :], 0
        ),
        -1,
    )

    end_kv = sds((batches, BLOCK, 6 * HD), BF16)
    end_all = sds((batches, BLOCK, 10 * HD), BF16)
    sent, kv_low, kv_high = call(
        partial(dispatch_kernel, bd),
        (sds((slots, BLOCK, 6 * HD), BF16), end_kv, end_kv),
        name="dispatch",
    )(kv_blocks, smem=(source_of,))
    rand_kv = to_owners(after(sent, arrived))
    up = [(i, i + 1) for i in range(devices - 1)]
    down = [(b, a) for a, b in up]
    low = lax.ppermute(kv_high, "seq", up)
    high = lax.ppermute(kv_low, "seq", down)

    bias, seq_bias, column_bias, wo256 = call(
        partial(bias_kernel, bd, blocks_all),
        (
            sds((total, 1, 8 * BLOCK), F32),
            sds((batches, 1, per), F32),
            sds((total, BLOCK, 4 * HD), F32),
            sds((width, 4 * HD), BF16),
        ),
        name="bias",
    )(key_keep.reshape(batches * blocks_all, BLOCK), w_out, smem=(mine, meta))

    grad_up = dot_nn(out_grad.reshape(batches * per, width), w_down)
    grad_up = grad_up.reshape(batches, per, hidden_here)

    part = sds((batches, BLOCK, 4 * HD), F32)
    low_piece = sds((piece, width), BF16)
    low_pieces = sds((groups * piece, width), BF16)
    high_piece = sds((piece, width), F32)
    attn, lse = [], []

    def attend(g):
        half_of = lambda array: part_of(array, g, groups)
        out, stat = call(
            partial(sparse_fwd_kernel, g * seqs * bd, seqs, per, share),
            (sds((4 * piece, 4 * HD), BF16), sds((seqs * per, 2 * HD), F32)),
            (
                pltpu.VMEM((seqs, per + 2 * BLOCK, 6 * HD), BF16),
                pltpu.VMEM((2, 8 * BLOCK, 6 * HD), BF16),
            ),
            name="sparse_fwd",
        )(
            half_of(q_blocks), half_of(kv_seqs), half_of(low), half_of(high), half_of(lead0), half_of(lead1),
            rand_kv, half_of(bias), smem=(slot_of, meta),
        )
        attn.append(out)
        lse.append(stat)

    lead_rows = sds((batches * BLOCK, width), BF16)
    lead_first0, lead_first1, lead0, lead1, part_mine, part_given = call(
        lead_fwd_kernel, (lead_rows, lead_rows, end_all, end_all, part, part), name="lead_fwd"
    )(kv_seqs, after(seq_bias, grad_up), lead_x0, lead_x1, norm1_gain, norm1_shift, w640, smem=(meta,))
    part_got = collect_first(part_given, devices)
    q_slots = call(gather_kernel, sds((slots, BLOCK, 4 * HD), BF16), name="gather")(q_blocks, smem=(query_of,))
    rand_q = to_owners(after(q_slots, rand_kv, part_got, low, high))
    attend(0)
    lead_parts = collect_rest(merge(part_mine, part_got), devices, merge)
    attend(1)
    lead_out, lead_lse = call(
        lead_finish_kernel,
        (sds(part.shape, BF16), sds((batches, BLOCK, 2 * HD), F32)),
        name="lead_finish",
        limit=SMALL,
    )(*lead_parts)
    out = call(
        partial(out_project_kernel, groups, seqs, per, share),
        (sds((4 * piece, 4 * HD), BF16),) * groups + (low_piece,) * (4 * groups),
        name="out_project",
        limit=SMALL,
    )(wo256, lead_out, *attn, smem=(meta,))
    mixed = out[:groups]
    attn_parts = [scatter_tp(out[groups + 4 * g : groups + 4 * g + 4]) for g in range(groups)]

    flat = lambda lists: [v for group in lists for v in group]
    hidden, act, total_grad, sums2, attn_grad = [], [], [], [], []
    ups, pres, back_parts, down_parts = [], [], [], []
    for g in range(groups):
        h, a = share_call(mid_fwd_kernel, (high_piece, low_piece), [(layer_input, g, 0)], "mid_fwd")(
            meta, seqs, share, *attn_parts[g], norm2_gain, norm2_shift
        )
        hidden.append(h)
        act.append(gather_tp(a, attn_parts[-1][2:]))
    low_hidden = sds((piece, hidden_here), BF16)
    for g in range(groups):
        out = share_call(
            ffn_kernel, (low_hidden, low_hidden, low_piece) * 4, [(grad_up, g, k) for k in range(4)], "ffn", MIDDLE
        )(meta, seqs, share, *act[g], w_up)
        ups.append(out[0::3])
        pres.append(out[1::3])
        back_parts.append(scatter_tp(out[2::3]))
    for g in range(groups):
        t, a, s = share_call(
            mid_bwd_kernel, (high_piece, low_piece, sds((2, width), F32)), [(out_grad, g, 0)], "mid_bwd"
        )(meta, seqs, share, *back_parts[g], hidden[g], norm2_gain)
        total_grad.append(t)
        sums2.append(s)
        if g == 0:
            down_parts = call(partial(down_kernel, groups), (low_pieces,) * 4, name="down", limit=MIDDLE)(*flat(ups), w_down)
            attn_grad.append(gather_tp(a))
        if g == groups - 1:
            halves = sds((devices // 2, rows, hidden_here), BF16)
            ff_keep0, ff_send0, ff_keep1, ff_send1 = call(
                partial(ffn_grad_kernel, groups, seqs, per, share),
                (halves,) * 4,
                (
                    pltpu.VMEM((batches * per, width), BF16),
                    pltpu.VMEM((batches * per, hidden_here), BF16),
                    pltpu.VMEM((width, 2 * hidden_here), F32),
                ),
                name="ffn_grad",
                limit=MIDDLE,
            )(
                out_grad.reshape(batches * per, width), *flat(ups), *flat(act), *flat(pres), smem=(meta,)
            )
            attn_grad.append(gather_tp(a, (), (ff_send0,)))
            ff_got0 = sum_seq_first(after(ff_send0, attn_grad[-1][1]), devices)

    lead_grad = call(
        partial(lead_grad_kernel, groups, seqs, per, share),
        sds((batches, BLOCK, 4 * HD), BF16),
        (pltpu.VMEM((batches * BLOCK, width), BF16),),
        name="lead_grad",
        limit=SMALL,
    )(wo256, lead_lse, lead_out, *flat(attn_grad), smem=(meta,))
    grads, sent = call(
        partial(heads_grad_kernel, groups, seqs, per, share),
        (sds((batches * per, 4 * HD), BF16), sds((slots, BLOCK, 4 * HD), BF16)),
        name="heads_grad",
        limit=MIDDLE,
    )(wo256, *flat(attn_grad), *mixed, *lse, smem=(query_of, meta))
    *lead_do, arrived = spread(lead_grad, myself, devices, sent)
    rand_do = to_owners(after(sent, arrived, rand_q, ff_got0))
    ff_got1 = sum_seq_first(after(ff_send1, arrived), devices)
    dend = sds(end_kv.shape, F32)
    dq, dkv, ret_low, ret_high, dlead0, dlead1 = call(
        partial(sparse_bwd_kernel, batches, per),
        (sds((total, BLOCK, 4 * HD), F32), sds((batches, per, 6 * HD), F32), end_kv, end_kv, dend, dend),
        (
            pltpu.VMEM((batches, per + 2 * BLOCK, 6 * HD), BF16),
            pltpu.VMEM((2, 8 * BLOCK, 6 * HD), BF16),
            pltpu.VMEM((batches, per + 2 * BLOCK, 6 * HD), F32),
            pltpu.VMEM((batches, 2 * BLOCK, 6 * HD), F32),
        ),
        name="sparse_bwd",
    )(
        q_blocks, kv_seqs, low, high, lead0, lead1, rand_kv, bias,
        after(grads, *lead_do).reshape(total, BLOCK, 4 * HD), smem=(slot_of,),
    )
    from_low = lax.ppermute(ret_high, "seq", up)
    from_high = lax.ppermute(ret_low, "seq", down)
    dkv, ends_mine, ends_given = call(
        lead_bwd_kernel, (sds((batches, per, 6 * HD), F32), end_all, end_all), name="lead_bwd"
    )(lead0, lead1, kv_seqs, seq_bias, dkv, dlead0, dlead1, *lead_do, smem=(meta,))
    add = lambda a, b: (a.astype(F32) + b.astype(F32)).astype(BF16)
    ends_first = collect_first(ends_given, devices)
    ends_got = collect_rest(add(after(ends_mine, from_low, from_high), ends_first), devices, add)

    dkv = call(slots_kernel, sds((total, BLOCK, 6 * HD), F32), name="slots")(
        rand_q, rand_do, kv_blocks, column_bias,
        dkv.reshape(total, BLOCK, 6 * HD), smem=(source_of, valid),
    )
    ff_half = jnp.concatenate(
        [
            (keep.astype(F32) + got.astype(F32)).astype(BF16)
            for keep, got in ((ff_keep0, ff_got0), (after(ff_keep1, dkv), after(ff_got1, dkv)))
        ],
        2,
    )
    ff = across(after(ff_half, *ends_got), devices)
    halves = sds((devices // 2, rows, 14 * HD), BF16)
    *first_back, qkv_keep, qkv_send = call(
        partial(tail_kernel, groups, seqs, per, share, devices),
        (low_pieces,) * 4 + (halves, halves),
        (
            pltpu.VMEM((total * BLOCK, 10 * HD), BF16),
            pltpu.VMEM((width, 14 * HD), F32),
            pltpu.VMEM((4 * piece, width), BF16),
        ),
        name="tail",
    )(
        dq, dkv, from_low, from_high, first, lead_first0, lead_first1, ends_mine, ends_given,
        *flat(attn_grad), *mixed, w640, norm1_gain, norm1_shift, *sums2, *ends_got, smem=(meta,),
    )
    qkv_got = sum_seq_first(qkv_send, devices)
    terms = scatter_tp(first_back)
    out_terms = scatter_tp([after(part, first_back[0]) for part in down_parts])
    ff = sum_of(ff)
    gq = sum_seq_rest([(qkv_keep, after(qkv_got, ff))], meta, devices)
    input_grad = share_call(
        partial(end_kernel, groups),
        sds((batches, share, width), F32),
        [(layer_input, g, 0) for g in range(groups)],
        "end",
    )(meta, seqs, share, *terms, *total_grad, norm1_gain)
    layer_output = call(
        partial(output_kernel, groups), sds((batches, share, width), F32), name="output", limit=SMALL
    )(*out_terms, *hidden)

    g_down, g_up = ff[:, :hidden_here], ff[:, hidden_here:]
    gq = sum_of(gq)
    norms = gq[:, HD : 2 * HD]
    norms = norms + swap_tp(norms, 1)
    norms = norms + swap_tp(norms, 2)
    g_out = jnp.concatenate([gq[:, 10 * HD : 12 * HD], gq[:, 13 * HD :]], 1)
    g_qkv = jnp.stack(
        [
            jnp.concatenate([gq[:, 2 * HD : 4 * HD], gq[:, :HD]], 1) * scale,
            jnp.concatenate([gq[:, 8 * HD : 10 * HD], gq[:, 6 * HD : 7 * HD]], 1),
            jnp.concatenate([gq[:, 4 * HD : 6 * HD], gq[:, 7 * HD : 8 * HD]], 1),
        ],
        1,
    )
    return (
        layer_output, input_grad, g_qkv, g_out, g_up, g_down, norms[:, 0], norms[:, 1], norms[:, 2], norms[:, 3],
    )


def solution(mesh):
    return jax.shard_map(
        per_device,
        mesh=mesh,
        in_specs=(
            P(None, "seq", None),
            P(None, "seq", None),
            P(),
            P(),
            P(None, None, "tp"),
            P(None, "tp"),
            P(),
            P(),
            P(None, "tp"),
            P(None, "tp"),
            P(),
            P(),
        ),
        out_specs=(
            P(None, ("seq", "tp"), None),
            P(None, ("seq", "tp"), None),
            P("seq", None, "tp"),
            P("seq", "tp"),
            P("seq", "tp"),
            P("seq", "tp"),
            P("seq"),
            P("seq"),
            P("seq"),
            P("seq"),
        ),
        check_vma=False,
    )
```

profile of v0, /device:TPU:0, one launch (start us, length us, event | category | flops | bytes accessed | tf_op | source)
XLA Modules:
  0.0 326.4 jit_solution(12090505902558605650)
XLA Ops:
  1.7 4.9 %collective-permute-start = (bf16[2,64,768]{2,1,0:T(8,128)(2,1)S(1)}, bf16[2,64,768]{2,1,0:T(8,128)(2,1)S(1)}, u32[]{:S(2)}, u32[]{:S(2)}) collective-permute-start(bf16[2,64,768]{2,1,0:T(8,128)(2,1)S(1)} %select_select_fusion), channel_id=1, source_target_pairs={{0,4},{28,24},{1,5},{29,25},{2,6},{30,26},{3,7},{31,27}} | collective-permute-start | bytes 589832 | tf_op jit(solution)/shard_map/ppermute | solution.py:841
  12.4 6.0 %project.1 = (bf16[1024,768]{1,0:T(8,128)(2,1)}, bf16[1024,256]{1,0:T(8,128)(2,1)}, bf16[1024,384]{1,0:T(8,128)(2,1)}, bf16[768,640]{1,0:T(8,128)(2,1)}) custom-call(bf16[1024,768]{1,0:T(8,128)(2,1)} %bitcast.34, f32[768]{0:T(1024)} %refs_7_.1, f32[768]{0:T(1024)} %refs_12_.1, bf16[3,768,192]{2,1,0:T(8,128)(2,1)} %bitcast.48), custom_call_target="tpu_custom_call" | custom-call | bytes 10500000 | tf_op jit(solution)/shard_map/project/pallas_call | solution.py:224
  29.5 5.0 %all-to-all-start = ((bf16[48,64,384]{2,1,0:T(8,128)(2,1)}), bf16[48,64,384]{2,1,0:T(8,128)(2,1)}, u32[]{:S(2)}, u32[]{:S(2)}) async-start(bf16[48,64,384]{2,1,0:T(8,128)(2,1)} %get-tuple-element.173), calls=%async_computation | async-start | bytes 4718592 | tf_op jit(solution)/shard_map/all_to_all | solution.py:873
  34.5 3.9 %collective-permute-start.4 = (bf16[2,64,384]{2,1,0:T(8,128)(2,1)}, bf16[2,64,384]{2,1,0:T(8,128)(2,1)S(1)}, u32[]{:S(2)}, u32[]{:S(2)}) collective-permute-start(bf16[2,64,384]{2,1,0:T(8,128)(2,1)} %get-tuple-element.169), channel_id=1, source_target_pairs={{0,4},{4,8},{8,12},{12,16},{16,20},{20,24},{24,28},{1,5},{5,9},{9,... | collective-permute-start | bytes 294920 | tf_op jit(solution)/shard_map/ppermute | solution.py:997
  49.3 3.8 %lead_fwd.1 = (bf16[128,768]{1,0:T(8,128)(2,1)}, bf16[128,768]{1,0:T(8,128)(2,1)}, bf16[2,64,640]{2,1,0:T(8,128)(2,1)}, bf16[2,64,640]{2,1,0:T(8,128)(2,1)}, f32...) custom-call(s32[5]{0:T(128)} %stack.45.meta_ref, bf16[2,512,384]{2,1,0:T(8,128)(2,1)} %bitcast.38, ...), custom_call_target="tpu_custom_call" | custom-call | bytes 7000000 | tf_op jit(solution)/shard_map/lead_fwd/pallas_call | solution.py:91
  53.1 5.3 %collective-permute-start.6 = (f32[2,64,256]{2,1,0:T(8,128)}, f32[2,64,256]{2,1,0:T(8,128)S(1)}, u32[]{:S(2)}, u32[]{:S(2)}) collective-permute-start(f32[2,64,256]{2,1,0:T(8,128)} %get-tuple-element.176), channel_id=1, source_target_pairs={{12,4},{20,16},{24,8},{28,0},{16,24},{8,12},{4,20},{0,28},{13,5},{... | collective-permute-start | bytes 393224 | tf_op jit(solution)/shard_map/ppermute | solution.py:857
  61.5 29.5 %all-to-all-done.rand_ref = bf16[48,64,384]{2,1,0:T(8,128)(2,1)} async-done(((bf16[48,64,384]{2,1,0:T(8,128)(2,1)}), bf16[48,64,384]{2,1,0:T(8,128)(2,1)}, u32[]{:S(2)}, u32[]{:S(2)}) %all-to-all-start) | async-done | bytes 2359328 | tf_op jit(solution)/shard_map/all_to_all | solution.py:873
  91.1 5.7 %sparse_fwd.2 = (bf16[512,256]{1,0:T(8,128)(2,1)}, f32[512,128]{1,0:T(8,128)}) custom-call(s32[48]{0:T(128)} %copy-done.71, s32[5]{0:T(128)} %stack.45.meta_ref, bf16[16,64,256]{2,1,0:T(8,128)(2,1)} %bitcast.45, bf16[2,512,384]{2,1,0:T(8,128)(2,1)} %bitcast.39, bf16[2,64,384]{2,1,0:T(8,128)(2,1)} %copy-done.57, bf16[2,64,384]{2,1,0:T(8,128)(2,1)} %copy-done.58, ...), custom_call_target="tpu_custom_call" | custom-call | bytes 12250000 | tf_op jit(solution)/shard_map/sparse_fwd/pallas_call | solution.py:91
  101.3 5.7 %sparse_fwd.3 = (bf16[512,256]{1,0:T(8,128)(2,1)}, f32[512,128]{1,0:T(8,128)}) custom-call(s32[48]{0:T(128)} %copy-done.71, s32[5]{0:T(128)} %stack.45.meta_ref, bf16[16,64,256]{2,1,0:T(8,128)(2,1)} %bitcast.46, bf16[2,512,384]{2,1,0:T(8,128)(2,1)} %bitcast.40, bf16[2,64,384]{2,1,0:T(8,128)(2,1)} %copy-done.57, bf16[2,64,384]{2,1,0:T(8,128)(2,1)} %copy-done.58, ...), custom_call_target="tpu_custom_call" | custom-call | bytes 12250000 | tf_op jit(solution)/shard_map/sparse_fwd/pallas_call | solution.py:91
  118.3 4.6 %all-to-all-start.1 = ((bf16[48,64,256]{2,1,0:T(8,128)(2,1)}), bf16[48,64,256]{2,1,0:T(8,128)(2,1)}, u32[]{:S(2)}, u32[]{:S(2)}) async-start(bf16[48,64,256]{2,1,0:T(8,128)(2,1)} %gather.1), calls=%async_computation.1 | async-start | bytes 3145728 | tf_op jit(solution)/shard_map/all_to_all | solution.py:873
  127.8 4.6 %collective-permute-done.12.y_ref = bf16[128,768]{1,0:T(8,128)(2,1)S(1)} collective-permute-done((bf16[128,768]{1,0:T(8,128)(2,1)S(1)}, bf16[128,768]{1,0:T(8,128)(2,1)S(1)}, u32[]{:S(2)}, u32[]{:S(2)}) %collective-permute-start.12) | collective-permute-done | bytes 196640 | tf_op jit(solution)/shard_map/ppermute | solution.py:808
  139.0 4.9 %collective-permute-done.16.refs_5_.refs_9_ = bf16[128,768]{1,0:T(8,128)(2,1)S(1)} collective-permute-done((bf16[128,768]{1,0:T(8,128)(2,1)S(1)}, bf16[128,768]{1,0:T(8,128)(2,1)S(1)}, u32[]{:S(2)}, u32[]{:S(2)}) %collective-permute-start.16) | collective-permute-done | bytes 196640 | tf_op jit(solution)/shard_map/ppermute | solution.py:808
  156.3 5.3 %collective-permute-done.24.y_ref = bf16[128,768]{1,0:T(8,128)(2,1)S(1)} collective-permute-done((bf16[128,768]{1,0:T(8,128)(2,1)S(1)}, bf16[128,768]{1,0:T(8,128)(2,1)S(1)}, u32[]{:S(2)}, u32[]{:S(2)}) %collective-permute-start.24) | collective-permute-done | bytes 196640 | tf_op jit(solution)/shard_map/ppermute | solution.py:808
  193.7 3.8 %collective-permute-done.37 = bf16[2,64,256]{2,1,0:T(8,128)(2,1)S(1)} collective-permute-done((bf16[2,64,256]{2,1,0:T(8,128)(2,1)S(1)}, bf16[2,64,256]{2,1,0:T(8,128)(2,1)S(1)}, u32[]{:S(2)}, u32[]{:S(2)}) %collective-permute-start.37) | collective-permute-done | bytes 65568 | tf_op jit(solution)/shard_map/ppermute | solution.py:843
  197.5 4.5 %all-to-all-start.2 = ((bf16[48,64,256]{2,1,0:T(8,128)(2,1)}), bf16[48,64,256]{2,1,0:T(8,128)(2,1)}, u32[]{:S(2)}, u32[]{:S(2)}) async-start(bf16[48,64,256]{2,1,0:T(8,128)(2,1)} %get-tuple-element.258), calls=%async_computation.2 | async-start | bytes 3145728 | tf_op jit(solution)/shard_map/all_to_all | solution.py:873
  202.7 12.1 %sparse_bwd.1 = (f32[16,64,256]{2,1,0:T(8,128)}, f32[2,512,384]{2,1,0:T(8,128)}, bf16[2,64,384]{2,1,0:T(8,128)(2,1)}, bf16[2,64,384]{2,1,0:T(8,128)(2,1)}, f32[2,64,384]{2,1,0:T(8,128)}, /*index=5*/f32[2,64,384]{2,1,0:T(8,128)}) custom-call(s32[48]{0:T(128)} %copy-done.71, bf16[16,64,256]{2,1,0:T(8,128)(2,1)} %bitcast.47, bf16[2,512,384]{2,1,0:T(8,128)(2,1)} %bitcast.41, ...), custom_call_target="tpu_custom_call" | custom-call | bytes 22750000 | tf_op jit(solution)/shard_map/sparse_bwd/pallas_call | solution.py:91
  214.8 4.9 %lead_bwd.1 = (f32[2,512,384]{2,1,0:T(8,128)}, bf16[2,64,640]{2,1,0:T(8,128)(2,1)}, bf16[2,64,640]{2,1,0:T(8,128)(2,1)}) custom-call(s32[5]{0:T(128)} %stack.45.meta_ref, bf16[2,64,640]{2,1,0:T(8,128)(2,1)} %get-tuple-element.171.lead0_ref, bf16[2,64,640]{2,1,0:T(8,128)(2,1)} %get-tuple-element.172.lead1_ref, bf16[2,512,384]{2,1,0:T(8,128)(2,1)} %bitcast.42, ...), custom_call_target="tpu_custom_call" | custom-call | bytes 8750000 | tf_op jit(solution)/shard_map/lead_bwd/pallas_call | solution.py:91
  219.6 4.7 %collective-permute-start.41 = (bf16[2,64,640]{2,1,0:T(8,128)(2,1)}, bf16[2,64,640]{2,1,0:T(8,128)(2,1)S(1)}, u32[]{:S(2)}, u32[]{:S(2)}) collective-permute-start(bf16[2,64,640]{2,1,0:T(8,128)(2,1)} %get-tuple-element.265.given_ref), channel_id=1, source_target_pairs={{12,4},{20,16},{24,8},{28,0},{16,24},{8,12},{4,20},{0,28},{13,5},{... | collective-permute-start | bytes 491528 | tf_op jit(solution)/shard_map/ppermute | solution.py:857
  230.6 5.1 %collective-permute-done.40.ret_high_ref = bf16[2,64,384]{2,1,0:T(8,128)(2,1)S(1)} collective-permute-done((bf16[2,64,384]{2,1,0:T(8,128)(2,1)S(1)}, bf16[2,64,384]{2,1,0:T(8,128)(2,1)S(1)}, u32[]{:S(2)}, u32[]{:S(2)}) %collective-permute-start.40) | collective-permute-done | bytes 98336 | tf_op jit(solution)/shard_map/ppermute | solution.py:1138
  243.3 15.2 %slots.1.dkv_ref = f32[16,64,384]{2,1,0:T(8,128)} custom-call(s32[48]{0:T(128)} %reshape.233.index_ref, s32[48]{0:T(128)} %reshape.241.valid_ref, bf16[48,64,256]{2,1,0:T(8,128)(2,1)} %all-to-all-done.1.q_got_ref, bf16[48,64,256]{2,1,0:T(8,128)(2,1)} %all-to-all-done.2.do_got_ref, bf16[16,64,384]{2,1,0:T(8,128)(2,1)} %bitcast.43, ...), custom_call_target="tpu_custom_call" | custom-call | bytes 24500000 | tf_op jit(solution)/shard_map/slots/pallas_call | solution.py:91
  260.9 10.1 %all-to-all-start.3 = ((bf16[4,96,1536]{2,1,0:T(8,128)(2,1)}), bf16[4,96,1536]{2,1,0:T(8,128)(2,1)}, u32[]{:S(2)}, u32[]{:S(2)}) async-start(bf16[4,96,1536]{2,1,0:T(8,128)(2,1)} %pad_maximum_fusion), calls=%async_computation.3 | async-start | bytes 2359296 | tf_op jit(solution)/shard_map/all_to_all | solution.py:898
  271.0 10.8 %tail.1 = (bf16[256,768]{1,0:T(8,128)(2,1)}, bf16[256,768]{1,0:T(8,128)(2,1)}, bf16[256,768]{1,0:T(8,128)(2,1)}, bf16[256,768]{1,0:T(8,128)(2,1)}, bf16[4,96,896...) custom-call(s32[5]{0:T(128)} %stack.45.meta_ref, f32[16,64,256]{2,1,0:T(8,128)} %get-tuple-element.249.dq_ref, ...), custom_call_target="tpu_custom_call" | custom-call | bytes 8750000 | tf_op jit(solution)/shard_map/tail/pallas_call | solution.py:91
  288.3 12.0 %all-to-all-done.3 = bf16[4,96,1536]{2,1,0:T(8,128)(2,1)} async-done(((bf16[4,96,1536]{2,1,0:T(8,128)(2,1)}), bf16[4,96,1536]{2,1,0:T(8,128)(2,1)}, u32[]{:S(2)}, u32[]{:S(2)}) %all-to-all-start.3) | async-done | bytes 1179680 | tf_op jit(solution)/shard_map/all_to_all | solution.py:898
  315.5 4.5 %collective-permute-done.54 = bf16[96,896]{1,0:T(8,128)(2,1)S(1)} collective-permute-done((bf16[96,896]{1,0:T(8,128)(2,1)}, bf16[96,896]{1,0:T(8,128)(2,1)S(1)}, u32[]{:S(2)}, u32[]{:S(2)}) %collective-permute-start.54) | collective-permute-done | bytes 172064 | tf_op jit(solution)/shard_map/ppermute | solution.py:889
  (327 shorter events, 147.8 us)
Async XLA Ops:
  1.7 16.7 %collective-permute-start = (bf16[2,64,768]{2,1,0:T(8,128)(2,1)S(1)}, bf16[2,64,768]{2,1,0:T(8,128)(2,1)S(1)}, u32[]{:S(2)}, u32[]{:S(2)}) collective-permute-start(bf16[2,64,768]{2,1,0:T(8,128)(2,1)S(1)} %select_select_fusion), channel_id=1, source_target_pairs={{0,4},{28,24},{1,5},{29,25},{2,6},{30,26},{3,7},{31,27}} | collective-permute-start | bytes 589832 | tf_op jit(solution)/shard_map/ppermute | solution.py:841
  6.6 11.9 %collective-permute-start.1 = (bf16[2,64,768]{2,1,0:T(8,128)(2,1)S(1)}, bf16[2,64,768]{2,1,0:T(8,128)(2,1)S(1)}, u32[]{:S(2)}, u32[]{:S(2)}) collective-permute-start(bf16[2,64,768]{2,1,0:T(8,128)(2,1)S(1)} %select_select_fusion), channel_id=1, source_target_pairs={{0,8},{28,20},{1,9},{29,21},{2,10},{30,22},{3,11},{31,23}} | collective-permute-start | bytes 589832 | tf_op jit(solution)/shard_map/ppermute | solution.py:841
  29.5 61.6 %all-to-all-start = ((bf16[48,64,384]{2,1,0:T(8,128)(2,1)}), bf16[48,64,384]{2,1,0:T(8,128)(2,1)}, u32[]{:S(2)}, u32[]{:S(2)}) async-start(bf16[48,64,384]{2,1,0:T(8,128)(2,1)} %get-tuple-element.173), calls=%async_computation | async-start | bytes 4718592 | tf_op jit(solution)/shard_map/all_to_all | solution.py:873
  34.5 27.1 %collective-permute-start.4 = (bf16[2,64,384]{2,1,0:T(8,128)(2,1)}, bf16[2,64,384]{2,1,0:T(8,128)(2,1)S(1)}, u32[]{:S(2)}, u32[]{:S(2)}) collective-permute-start(bf16[2,64,384]{2,1,0:T(8,128)(2,1)} %get-tuple-element.169), channel_id=1, source_target_pairs={{0,4},{4,8},{8,12},{12,16},{16,20},{20,24},{24,28},{1,5},{5,9},{9,... | collective-permute-start | bytes 294920 | tf_op jit(solution)/shard_map/ppermute | solution.py:997
  38.4 23.1 %collective-permute-start.5 = (bf16[2,64,384]{2,1,0:T(8,128)(2,1)}, bf16[2,64,384]{2,1,0:T(8,128)(2,1)S(1)}, u32[]{:S(2)}, u32[]{:S(2)}) collective-permute-start(bf16[2,64,384]{2,1,0:T(8,128)(2,1)} %get-tuple-element.170), channel_id=1, source_target_pairs={{4,0},{8,4},{12,8},{16,12},{20,16},{24,20},{28,24},{5,1},{9,5},{13... | collective-permute-start | bytes 294920 | tf_op jit(solution)/shard_map/ppermute | solution.py:998
  53.1 43.7 %collective-permute-start.6 = (f32[2,64,256]{2,1,0:T(8,128)}, f32[2,64,256]{2,1,0:T(8,128)S(1)}, u32[]{:S(2)}, u32[]{:S(2)}) collective-permute-start(f32[2,64,256]{2,1,0:T(8,128)} %get-tuple-element.176), channel_id=1, source_target_pairs={{12,4},{20,16},{24,8},{28,0},{16,24},{8,12},{4,20},{0,28},{13,5},{... | collective-permute-start | bytes 393224 | tf_op jit(solution)/shard_map/ppermute | solution.py:857
  118.3 79.3 %all-to-all-start.1 = ((bf16[48,64,256]{2,1,0:T(8,128)(2,1)}), bf16[48,64,256]{2,1,0:T(8,128)(2,1)}, u32[]{:S(2)}, u32[]{:S(2)}) async-start(bf16[48,64,256]{2,1,0:T(8,128)(2,1)} %gather.1), calls=%async_computation.1 | async-start | bytes 3145728 | tf_op jit(solution)/shard_map/all_to_all | solution.py:873
  153.7 12.6 %collective-permute-start.25 = (bf16[128,768]{1,0:T(8,128)(2,1)S(1)}, bf16[128,768]{1,0:T(8,128)(2,1)S(1)}, u32[]{:S(2)}, u32[]{:S(2)}) collective-permute-start(bf16[128,768]{1,0:T(8,128)(2,1)S(1)} %get-tuple-element.220), channel_id=1, source_target_pairs={{0,1},{1,0},{2,3},{3,2},{4,5},{5,4},{6,7},{7,6},{8,9},{9,8},{10,11... | collective-permute-start | bytes 589832 | tf_op jit(solution)/shard_map/ppermute | solution.py:808
  175.8 21.7 %collective-permute-start.38 = (bf16[4,96,768]{2,1,0:T(8,128)(2,1)S(1)}, bf16[4,96,768]{2,1,0:T(8,128)(2,1)}, u32[]{:S(2)}, u32[]{:S(2)}) collective-permute-start(bf16[4,96,768]{2,1,0:T(8,128)(2,1)S(1)} %get-tuple-element.257), channel_id=1, source_target_pairs={{0,4},{4,0},{8,12},{12,8},{16,20},{20,16},{24,28},{28,24},{1,5},{5... | collective-permute-start | bytes 1769480 | tf_op jit(solution)/shard_map/ppermute | solution.py:877
  197.5 45.7 %all-to-all-start.2 = ((bf16[48,64,256]{2,1,0:T(8,128)(2,1)}), bf16[48,64,256]{2,1,0:T(8,128)(2,1)}, u32[]{:S(2)}, u32[]{:S(2)}) async-start(bf16[48,64,256]{2,1,0:T(8,128)(2,1)} %get-tuple-element.258), calls=%async_computation.2 | async-start | bytes 3145728 | tf_op jit(solution)/shard_map/all_to_all | solution.py:873
  219.6 16.7 %collective-permute-start.41 = (bf16[2,64,640]{2,1,0:T(8,128)(2,1)}, bf16[2,64,640]{2,1,0:T(8,128)(2,1)S(1)}, u32[]{:S(2)}, u32[]{:S(2)}) collective-permute-start(bf16[2,64,640]{2,1,0:T(8,128)(2,1)} %get-tuple-element.265.given_ref), channel_id=1, source_target_pairs={{12,4},{20,16},{24,8},{28,0},{16,24},{8,12},{4,20},{0,28},{13,5},{... | collective-permute-start | bytes 491528 | tf_op jit(solution)/shard_map/ppermute | solution.py:857
  227.2 31.2 %collective-permute-start.46 = (bf16[4,96,768]{2,1,0:T(8,128)(2,1)S(1)}, bf16[4,96,768]{2,1,0:T(8,128)(2,1)}, u32[]{:S(2)}, u32[]{:S(2)}) collective-permute-start(bf16[4,96,768]{2,1,0:T(8,128)(2,1)S(1)} %copy-done.50), channel_id=1, source_target_pairs={{0,4},{4,0},{8,12},{12,8},{16,20},{20,16},{24,28},{28,24},{1,5},{5... | collective-permute-start | bytes 1769480 | tf_op jit(solution)/shard_map/ppermute | solution.py:877
  237.4 23.5 %collective-permute-start.42 = (bf16[2,64,640]{2,1,0:T(8,128)(2,1)S(1)}, bf16[2,64,640]{2,1,0:T(8,128)(2,1)S(1)}, u32[]{:S(2)}, u32[]{:S(2)}) collective-permute-start(bf16[2,64,640]{2,1,0:T(8,128)(2,1)S(1)} %add_convert_fusion.8.refs_15_), channel_id=1, source_target_pairs={{4,0},{24,28},{5,1},{25,29},{6,2},{26,30},{7,3},{27,31}} | collective-permute-start | bytes 491528 | tf_op jit(solution)/shard_map/ppermute | solution.py:864
  238.7 22.2 %collective-permute-start.43 = (bf16[2,64,640]{2,1,0:T(8,128)(2,1)S(1)}, bf16[2,64,640]{2,1,0:T(8,128)(2,1)S(1)}, u32[]{:S(2)}, u32[]{:S(2)}) collective-permute-start(bf16[2,64,640]{2,1,0:T(8,128)(2,1)S(1)} %add_convert_fusion.8.refs_15_), channel_id=1, source_target_pairs={{8,0},{20,28},{9,1},{21,29},{10,2},{22,30},{11,3},{23,31}} | collective-permute-start | bytes 491528 | tf_op jit(solution)/shard_map/ppermute | solution.py:864
  240.0 20.9 %collective-permute-start.44 = (bf16[2,64,640]{2,1,0:T(8,128)(2,1)S(1)}, bf16[2,64,640]{2,1,0:T(8,128)(2,1)}, u32[]{:S(2)}, u32[]{:S(2)}) collective-permute-start(bf16[2,64,640]{2,1,0:T(8,128)(2,1)S(1)} %add_convert_fusion.8.refs_15_), channel_id=1, source_target_pairs={{16,0},{12,28},{17,1},{13,29},{18,2},{14,30},{19,3},{15,31}} | collective-permute-start | bytes 491528 | tf_op jit(solution)/shard_map/ppermute | solution.py:864
  260.9 39.5 %all-to-all-start.3 = ((bf16[4,96,1536]{2,1,0:T(8,128)(2,1)}), bf16[4,96,1536]{2,1,0:T(8,128)(2,1)}, u32[]{:S(2)}, u32[]{:S(2)}) async-start(bf16[4,96,1536]{2,1,0:T(8,128)(2,1)} %pad_maximum_fusion), calls=%async_computation.3 | async-start | bytes 2359296 | tf_op jit(solution)/shard_map/all_to_all | solution.py:898
  282.4 19.3 %collective-permute-start.45 = (bf16[4,96,896]{2,1,0:T(8,128)(2,1)}, bf16[4,96,896]{2,1,0:T(8,128)(2,1)}, u32[]{:S(2)}, u32[]{:S(2)}) collective-permute-start(bf16[4,96,896]{2,1,0:T(8,128)(2,1)} %get-tuple-element.273), channel_id=1, source_target_pairs={{0,4},{4,0},{8,12},{12,8},{16,20},{20,16},{24,28},{28,24},{1,5},{5... | collective-permute-start | bytes 2064392 | tf_op jit(solution)/shard_map/ppermute | solution.py:877
  282.9 30.6 %collective-permute-start.50 = (bf16[256,768]{1,0:T(8,128)(2,1)}, bf16[256,768]{1,0:T(8,128)(2,1)S(1)}, u32[]{:S(2)}, u32[]{:S(2)}) collective-permute-start(bf16[256,768]{1,0:T(8,128)(2,1)} %get-tuple-element.288), channel_id=1, source_target_pairs={{0,1},{1,0},{2,3},{3,2},{4,5},{5,4},{6,7},{7,6},{8,9},{9,8},{10,11... | collective-permute-start | bytes 1179656 | tf_op jit(solution)/shard_map/ppermute | solution.py:808
  282.9 21.4 %collective-permute-start.47 = (bf16[256,768]{1,0:T(8,128)(2,1)}, bf16[256,768]{1,0:T(8,128)(2,1)}, u32[]{:S(2)}, u32[]{:S(2)}) collective-permute-start(bf16[256,768]{1,0:T(8,128)(2,1)} %get-tuple-element.283), channel_id=1, source_target_pairs={{0,1},{1,0},{2,3},{3,2},{4,5},{5,4},{6,7},{7,6},{8,9},{9,8},{10,11... | collective-permute-start | bytes 1179656 | tf_op jit(solution)/shard_map/ppermute | solution.py:808
  284.5 29.1 %collective-permute-start.52 = (bf16[256,768]{1,0:T(8,128)(2,1)}, bf16[256,768]{1,0:T(8,128)(2,1)S(1)}, u32[]{:S(2)}, u32[]{:S(2)}) collective-permute-start(bf16[256,768]{1,0:T(8,128)(2,1)} %add_convert_fusion.2), channel_id=1, source_target_pairs={{0,2},{1,3},{2,0},{3,1},{4,6},{5,7},{6,4},{7,5},{8,10},{9,11},{10,... | collective-permute-start | bytes 1179656 | tf_op jit(solution)/shard_map/ppermute | solution.py:808
  287.8 18.9 %collective-permute-start.49 = (bf16[256,768]{1,0:T(8,128)(2,1)}, bf16[256,768]{1,0:T(8,128)(2,1)}, u32[]{:S(2)}, u32[]{:S(2)}) collective-permute-start(bf16[256,768]{1,0:T(8,128)(2,1)} %add_convert_fusion.3), channel_id=1, source_target_pairs={{0,2},{1,3},{2,0},{3,1},{4,6},{5,7},{6,4},{7,5},{8,10},{9,11},{10,... | collective-permute-start | bytes 1179656 | tf_op jit(solution)/shard_map/ppermute | solution.py:808
  304.0 11.5 %collective-permute-start.53 = (bf16[96,896]{1,0:T(8,128)(2,1)}, bf16[96,896]{1,0:T(8,128)(2,1)S(1)}, u32[]{:S(2)}, u32[]{:S(2)}) collective-permute-start(bf16[96,896]{1,0:T(8,128)(2,1)} %get-tuple-element.293), channel_id=1, source_target_pairs={{0,8},{4,12},{8,0},{12,4},{16,24},{20,28},{24,16},{28,20},{1,9},{5... | collective-permute-start | bytes 516104 | tf_op jit(solution)/shard_map/ppermute | solution.py:889
  304.3 15.6 %collective-permute-start.54 = (bf16[96,896]{1,0:T(8,128)(2,1)}, bf16[96,896]{1,0:T(8,128)(2,1)S(1)}, u32[]{:S(2)}, u32[]{:S(2)}) collective-permute-start(bf16[96,896]{1,0:T(8,128)(2,1)} %get-tuple-element.294), channel_id=1, source_target_pairs={{0,16},{4,20},{8,24},{12,28},{16,0},{20,4},{24,8},{28,12},{1,17},{... | collective-permute-start | bytes 516104 | tf_op jit(solution)/shard_map/ppermute | solution.py:889
  306.7 13.3 %collective-permute-start.55 = (bf16[96,896]{1,0:T(8,128)(2,1)}, bf16[96,896]{1,0:T(8,128)(2,1)S(1)}, u32[]{:S(2)}, u32[]{:S(2)}) collective-permute-start(bf16[96,896]{1,0:T(8,128)(2,1)} %get-tuple-element.295), channel_id=1, source_target_pairs={{0,24},{4,28},{8,16},{12,20},{16,8},{20,12},{24,0},{28,4},{1,25},{... | collective-permute-start | bytes 516104 | tf_op jit(solution)/shard_map/ppermute | solution.py:889
  (113 other events, 977.9 us)
where the time goes:
time: 328 us; the launch traced here: 326 us
  Pallas kernels  102 us (31%)
  starting transfers between devices  94.9 us (29%)
  waiting for transfers between devices  82.4 us (25%)
  local copies, waits for them, and re-layouts  23.3 us (7%)
  other arithmetic  18.6 us (6%)
    pallas_call x19, Pallas kernels, run(): pl.pallas_call(body, out_shape=outs, grid=(1,), in_specs=specs, out_specs...  83.9 us
    all_to_all x3, waiting for transfers between devices, to_owners(): return lax.all_to_all(slots, 'seq', split_axis=0, concat_axis=0, tiled=True)  29.5 us
    ppermute x32, waiting for transfers between devices, swap_tp(): lax.ppermute(value, 'tp', [(i, i ^ bit) for i in range(lax.axis_size('tp'...  24.9 us
    unnamed x152, local copies, waits for them, and re-layouts  17.8 us
    ppermute x32, starting transfers between devices, swap_tp(): lax.ppermute(value, 'tp', [(i, i ^ bit) for i in range(lax.axis_size('tp'...  16.2 us
    all_to_all x3, starting transfers between devices, to_owners(): return lax.all_to_all(slots, 'seq', split_axis=0, concat_axis=0, tiled=True)  14.1 us
    ppermute x6, starting transfers between devices, spread(): held = held + lax.ppermute(own, 'seq', mirrored([(0, k)], last))  13 us
    pallas_call x7, Pallas kernels, run(): pl.pallas_call(body, out_shape=outs, grid_spec=pltpu.PrefetchScalarGridSp...  12.4 us
  transfers between devices with their start and end apart: 62, of which 21 were waited for; matrix products, arithmetic and copies ran while one was open for 8% of the time, Pallas kernels for 30%

commit v1 on v0

--- a/solution.py
+++ b/solution.py
@@ -1054,7 +1054,6 @@
         partial(out_project_kernel, groups, seqs, per, share),
         (sds((4 * piece, 4 * HD), BF16),) * groups + (low_piece,) * (4 * groups),
         name="out_project",
-        limit=SMALL,
     )(wo256, lead_out, *attn, smem=(meta,))
     mixed = out[:groups]
     attn_parts = [scatter_tp(out[groups + 4 * g : groups + 4 * g + 4]) for g in range(groups)]

time: 328 us -> 323 us (0.985)
  local copies, waits for them, and re-layouts: 23.3 us -> 19 us
    unnamed x152 -> x128, local copies, waits for them, and re-layouts: 17.8 us -> 13.5 us
  transfers between devices with their start and end apart: 62 -> 62, of which waited for: 21 -> 22; matrix products, arithmetic and copies ran while one was open for 8% -> 8% of each run, Pallas kernels for 30% -> 31%
where the time goes in v1:
time: 323 us; the launch traced here: 322 us
  Pallas kernels  103 us (32%)
  starting transfers between devices  94.8 us (29%)
  waiting for transfers between devices  82.9 us (26%)
  local copies, waits for them, and re-layouts  19 us (6%)
  other arithmetic  17.1 us (5%)
    pallas_call x19, Pallas kernels, run(): pl.pallas_call(body, out_shape=outs, grid=(1,), in_specs=specs, out_specs...  85 us
    all_to_all x3, waiting for transfers between devices, to_owners(): return lax.all_to_all(slots, 'seq', split_axis=0, concat_axis=0, tiled=True)  29.6 us
    ppermute x32, waiting for transfers between devices, swap_tp(): lax.ppermute(value, 'tp', [(i, i ^ bit) for i in range(lax.axis_size('tp'...  26.3 us
    ppermute x32, starting transfers between devices, swap_tp(): lax.ppermute(value, 'tp', [(i, i ^ bit) for i in range(lax.axis_size('tp'...  16.3 us
    all_to_all x3, starting transfers between devices, to_owners(): return lax.all_to_all(slots, 'seq', split_axis=0, concat_axis=0, tiled=True)  14.1 us
    unnamed x128, local copies, waits for them, and re-layouts  13.5 us
    ppermute x6, starting transfers between devices, spread(): held = held + lax.ppermute(own, 'seq', mirrored([(0, k)], last))  13 us
    pallas_call x7, Pallas kernels, run(): pl.pallas_call(body, out_shape=outs, grid_spec=pltpu.PrefetchScalarGridSp...  12.4 us
  transfers between devices with their start and end apart: 62, of which 22 were waited for; matrix products, arithmetic and copies ran while one was open for 8% of the time, Pallas kernels for 31%

profile of v1, /device:TPU:0, one launch (start us, length us, event | category | flops | bytes accessed | tf_op | source)
XLA Modules:
  0.0 322.0 jit_solution(9361339857354904431)
XLA Ops:
  1.7 4.9 %collective-permute-start = (bf16[2,64,768]{2,1,0:T(8,128)(2,1)S(1)}, bf16[2,64,768]{2,1,0:T(8,128)(2,1)S(1)}, u32[]{:S(2)}, u32[]{:S(2)}) collective-permute-start(bf16[2,64,768]{2,1,0:T(8,128)(2,1)S(1)} %select_select_fusion), channel_id=1, source_target_pairs={{0,4},{28,24},{1,5},{29,25},{2,6},{30,26},{3,7},{31,27}} | collective-permute-start | bytes 589832 | tf_op jit(solution)/shard_map/ppermute | solution.py:841
  11.8 6.0 %project.1 = (bf16[1024,768]{1,0:T(8,128)(2,1)}, bf16[1024,256]{1,0:T(8,128)(2,1)}, bf16[1024,384]{1,0:T(8,128)(2,1)}, bf16[768,640]{1,0:T(8,128)(2,1)}) custom-call(bf16[1024,768]{1,0:T(8,128)(2,1)} %bitcast.34, f32[768]{0:T(1024)} %refs_7_.1, f32[768]{0:T(1024)} %refs_12_.1, bf16[3,768,192]{2,1,0:T(8,128)(2,1)} %bitcast.48), custom_call_target="tpu_custom_call" | custom-call | bytes 10500000 | tf_op jit(solution)/shard_map/project/pallas_call | solution.py:224
  28.9 5.0 %all-to-all-start = ((bf16[48,64,384]{2,1,0:T(8,128)(2,1)}), bf16[48,64,384]{2,1,0:T(8,128)(2,1)}, u32[]{:S(2)}, u32[]{:S(2)}) async-start(bf16[48,64,384]{2,1,0:T(8,128)(2,1)} %get-tuple-element.173), calls=%async_computation | async-start | bytes 4718592 | tf_op jit(solution)/shard_map/all_to_all | solution.py:873
  33.9 3.9 %collective-permute-start.4 = (bf16[2,64,384]{2,1,0:T(8,128)(2,1)}, bf16[2,64,384]{2,1,0:T(8,128)(2,1)S(1)}, u32[]{:S(2)}, u32[]{:S(2)}) collective-permute-start(bf16[2,64,384]{2,1,0:T(8,128)(2,1)} %get-tuple-element.169), channel_id=1, source_target_pairs={{0,4},{4,8},{8,12},{12,16},{16,20},{20,24},{24,28},{1,5},{5,9},{9,... | collective-permute-start | bytes 294920 | tf_op jit(solution)/shard_map/ppermute | solution.py:997
  48.8 3.8 %lead_fwd.1 = (bf16[128,768]{1,0:T(8,128)(2,1)}, bf16[128,768]{1,0:T(8,128)(2,1)}, bf16[2,64,640]{2,1,0:T(8,128)(2,1)}, bf16[2,64,640]{2,1,0:T(8,128)(2,1)}, f32...) custom-call(s32[5]{0:T(128)} %stack.45.meta_ref, bf16[2,512,384]{2,1,0:T(8,128)(2,1)} %bitcast.38, ...), custom_call_target="tpu_custom_call" | custom-call | bytes 7000000 | tf_op jit(solution)/shard_map/lead_fwd/pallas_call | solution.py:91
  52.6 5.3 %collective-permute-start.6 = (f32[2,64,256]{2,1,0:T(8,128)}, f32[2,64,256]{2,1,0:T(8,128)S(1)}, u32[]{:S(2)}, u32[]{:S(2)}) collective-permute-start(f32[2,64,256]{2,1,0:T(8,128)} %get-tuple-element.176), channel_id=1, source_target_pairs={{12,4},{20,16},{24,8},{28,0},{16,24},{8,12},{4,20},{0,28},{13,5},{... | collective-permute-start | bytes 393224 | tf_op jit(solution)/shard_map/ppermute | solution.py:857
  61.0 29.5 %all-to-all-done.rand_ref = bf16[48,64,384]{2,1,0:T(8,128)(2,1)} async-done(((bf16[48,64,384]{2,1,0:T(8,128)(2,1)}), bf16[48,64,384]{2,1,0:T(8,128)(2,1)}, u32[]{:S(2)}, u32[]{:S(2)}) %all-to-all-start) | async-done | bytes 2359328 | tf_op jit(solution)/shard_map/all_to_all | solution.py:873
  90.5 5.7 %sparse_fwd.2 = (bf16[512,256]{1,0:T(8,128)(2,1)}, f32[512,128]{1,0:T(8,128)}) custom-call(s32[48]{0:T(128)} %copy-done.60, s32[5]{0:T(128)} %stack.45.meta_ref, bf16[16,64,256]{2,1,0:T(8,128)(2,1)} %bitcast.45, bf16[2,512,384]{2,1,0:T(8,128)(2,1)} %bitcast.39, bf16[2,64,384]{2,1,0:T(8,128)(2,1)} %copy-done.44, bf16[2,64,384]{2,1,0:T(8,128)(2,1)} %copy-done.45, ...), custom_call_target="tpu_custom_call" | custom-call | bytes 12250000 | tf_op jit(solution)/shard_map/sparse_fwd/pallas_call | solution.py:91
  100.5 5.7 %sparse_fwd.3 = (bf16[512,256]{1,0:T(8,128)(2,1)}, f32[512,128]{1,0:T(8,128)}) custom-call(s32[48]{0:T(128)} %copy-done.60, s32[5]{0:T(128)} %stack.45.meta_ref, bf16[16,64,256]{2,1,0:T(8,128)(2,1)} %bitcast.46, bf16[2,512,384]{2,1,0:T(8,128)(2,1)} %bitcast.40, bf16[2,64,384]{2,1,0:T(8,128)(2,1)} %copy-done.44, bf16[2,64,384]{2,1,0:T(8,128)(2,1)} %copy-done.45, ...), custom_call_target="tpu_custom_call" | custom-call | bytes 12250000 | tf_op jit(solution)/shard_map/sparse_fwd/pallas_call | solution.py:91
  112.7 4.6 %all-to-all-start.1 = ((bf16[48,64,256]{2,1,0:T(8,128)(2,1)}), bf16[48,64,256]{2,1,0:T(8,128)(2,1)}, u32[]{:S(2)}, u32[]{:S(2)}) async-start(bf16[48,64,256]{2,1,0:T(8,128)(2,1)} %gather.1), calls=%async_computation.1 | async-start | bytes 3145728 | tf_op jit(solution)/shard_map/all_to_all | solution.py:873
  121.2 5.6 %collective-permute-done.12.y_ref = bf16[128,768]{1,0:T(8,128)(2,1)S(1)} collective-permute-done((bf16[128,768]{1,0:T(8,128)(2,1)S(1)}, bf16[128,768]{1,0:T(8,128)(2,1)S(1)}, u32[]{:S(2)}, u32[]{:S(2)}) %collective-permute-start.12) | collective-permute-done | bytes 196640 | tf_op jit(solution)/shard_map/ppermute | solution.py:808
  133.3 4.9 %collective-permute-done.16.refs_5_.refs_9_ = bf16[128,768]{1,0:T(8,128)(2,1)S(1)} collective-permute-done((bf16[128,768]{1,0:T(8,128)(2,1)S(1)}, bf16[128,768]{1,0:T(8,128)(2,1)S(1)}, u32[]{:S(2)}, u32[]{:S(2)}) %collective-permute-start.16) | collective-permute-done | bytes 196640 | tf_op jit(solution)/shard_map/ppermute | solution.py:808
  150.6 5.3 %collective-permute-done.24.y_ref = bf16[128,768]{1,0:T(8,128)(2,1)S(1)} collective-permute-done((bf16[128,768]{1,0:T(8,128)(2,1)S(1)}, bf16[128,768]{1,0:T(8,128)(2,1)S(1)}, u32[]{:S(2)}, u32[]{:S(2)}) %collective-permute-start.24) | collective-permute-done | bytes 196640 | tf_op jit(solution)/shard_map/ppermute | solution.py:808
  157.6 3.7 %down.1 = (bf16[256,768]{1,0:T(8,128)(2,1)S(1)}, bf16[256,768]{1,0:T(8,128)(2,1)S(1)}, bf16[256,768]{1,0:T(8,128)(2,1)}, bf16[256,768]{1,0:T(8,128)(2,1)S(1)}) custom-call(bf16[128,768]{1,0:T(8,128)(2,1)S(1)} %get-tuple-element.210.refs_0_, bf16[128,768]{1,0:T(8,128)(2,1)S(1)} %get-tuple-element.211.refs_1_, ...), custom_call_target="tpu_custom_call" | custom-call | bytes 10500000 | tf_op jit(solution)/shard_map/down/pallas_call | solution.py:91
  189.3 3.8 %collective-permute-done.37 = bf16[2,64,256]{2,1,0:T(8,128)(2,1)S(1)} collective-permute-done((bf16[2,64,256]{2,1,0:T(8,128)(2,1)S(1)}, bf16[2,64,256]{2,1,0:T(8,128)(2,1)S(1)}, u32[]{:S(2)}, u32[]{:S(2)}) %collective-permute-start.37) | collective-permute-done | bytes 65568 | tf_op jit(solution)/shard_map/ppermute | solution.py:843
  193.1 4.5 %all-to-all-start.2 = ((bf16[48,64,256]{2,1,0:T(8,128)(2,1)}), bf16[48,64,256]{2,1,0:T(8,128)(2,1)}, u32[]{:S(2)}, u32[]{:S(2)}) async-start(bf16[48,64,256]{2,1,0:T(8,128)(2,1)} %get-tuple-element.258), calls=%async_computation.2 | async-start | bytes 3145728 | tf_op jit(solution)/shard_map/all_to_all | solution.py:873
  198.2 12.1 %sparse_bwd.1 = (f32[16,64,256]{2,1,0:T(8,128)}, f32[2,512,384]{2,1,0:T(8,128)}, bf16[2,64,384]{2,1,0:T(8,128)(2,1)}, bf16[2,64,384]{2,1,0:T(8,128)(2,1)}, f32[2,64,384]{2,1,0:T(8,128)}, /*index=5*/f32[2,64,384]{2,1,0:T(8,128)}) custom-call(s32[48]{0:T(128)} %copy-done.60, bf16[16,64,256]{2,1,0:T(8,128)(2,1)} %bitcast.47, bf16[2,512,384]{2,1,0:T(8,128)(2,1)} %bitcast.41, ...), custom_call_target="tpu_custom_call" | custom-call | bytes 22750000 | tf_op jit(solution)/shard_map/sparse_bwd/pallas_call | solution.py:91
  210.3 4.8 %lead_bwd.1 = (f32[2,512,384]{2,1,0:T(8,128)}, bf16[2,64,640]{2,1,0:T(8,128)(2,1)}, bf16[2,64,640]{2,1,0:T(8,128)(2,1)}) custom-call(s32[5]{0:T(128)} %stack.45.meta_ref, bf16[2,64,640]{2,1,0:T(8,128)(2,1)} %get-tuple-element.171.lead0_ref, bf16[2,64,640]{2,1,0:T(8,128)(2,1)} %get-tuple-element.172.lead1_ref, bf16[2,512,384]{2,1,0:T(8,128)(2,1)} %bitcast.42, ...), custom_call_target="tpu_custom_call" | custom-call | bytes 8750000 | tf_op jit(solution)/shard_map/lead_bwd/pallas_call | solution.py:91
  215.1 4.7 %collective-permute-start.41 = (bf16[2,64,640]{2,1,0:T(8,128)(2,1)}, bf16[2,64,640]{2,1,0:T(8,128)(2,1)S(1)}, u32[]{:S(2)}, u32[]{:S(2)}) collective-permute-start(bf16[2,64,640]{2,1,0:T(8,128)(2,1)} %get-tuple-element.265.given_ref), channel_id=1, source_target_pairs={{12,4},{20,16},{24,8},{28,0},{16,24},{8,12},{4,20},{0,28},{13,5},{... | collective-permute-start | bytes 491528 | tf_op jit(solution)/shard_map/ppermute | solution.py:857
  226.1 5.2 %collective-permute-done.40.ret_high_ref = bf16[2,64,384]{2,1,0:T(8,128)(2,1)S(1)} collective-permute-done((bf16[2,64,384]{2,1,0:T(8,128)(2,1)S(1)}, bf16[2,64,384]{2,1,0:T(8,128)(2,1)S(1)}, u32[]{:S(2)}, u32[]{:S(2)}) %collective-permute-start.40) | collective-permute-done | bytes 98336 | tf_op jit(solution)/shard_map/ppermute | solution.py:1137
  238.4 15.2 %slots.1.dkv_ref = f32[16,64,384]{2,1,0:T(8,128)} custom-call(s32[48]{0:T(128)} %reshape.233.index_ref, s32[48]{0:T(128)} %reshape.241.valid_ref, bf16[48,64,256]{2,1,0:T(8,128)(2,1)} %all-to-all-done.1.q_got_ref, bf16[48,64,256]{2,1,0:T(8,128)(2,1)} %all-to-all-done.2.do_got_ref, bf16[16,64,384]{2,1,0:T(8,128)(2,1)} %bitcast.43, ...), custom_call_target="tpu_custom_call" | custom-call | bytes 24500000 | tf_op jit(solution)/shard_map/slots/pallas_call | solution.py:91
  256.0 10.6 %all-to-all-start.3 = ((bf16[4,96,1536]{2,1,0:T(8,128)(2,1)}), bf16[4,96,1536]{2,1,0:T(8,128)(2,1)}, u32[]{:S(2)}, u32[]{:S(2)}) async-start(bf16[4,96,1536]{2,1,0:T(8,128)(2,1)} %pad_maximum_fusion), calls=%async_computation.3 | async-start | bytes 2359296 | tf_op jit(solution)/shard_map/all_to_all | solution.py:898
  266.6 10.8 %tail.1 = (bf16[256,768]{1,0:T(8,128)(2,1)}, bf16[256,768]{1,0:T(8,128)(2,1)}, bf16[256,768]{1,0:T(8,128)(2,1)}, bf16[256,768]{1,0:T(8,128)(2,1)}, bf16[4,96,896...) custom-call(s32[5]{0:T(128)} %stack.45.meta_ref, f32[16,64,256]{2,1,0:T(8,128)} %get-tuple-element.249.dq_ref, ...), custom_call_target="tpu_custom_call" | custom-call | bytes 8750000 | tf_op jit(solution)/shard_map/tail/pallas_call | solution.py:91
  284.0 12.0 %all-to-all-done.3 = bf16[4,96,1536]{2,1,0:T(8,128)(2,1)} async-done(((bf16[4,96,1536]{2,1,0:T(8,128)(2,1)}), bf16[4,96,1536]{2,1,0:T(8,128)(2,1)}, u32[]{:S(2)}, u32[]{:S(2)}) %all-to-all-start.3) | async-done | bytes 1179680 | tf_op jit(solution)/shard_map/all_to_all | solution.py:898
  (303 shorter events, 142.8 us)
Async XLA Ops:
  1.7 16.2 %collective-permute-start = (bf16[2,64,768]{2,1,0:T(8,128)(2,1)S(1)}, bf16[2,64,768]{2,1,0:T(8,128)(2,1)S(1)}, u32[]{:S(2)}, u32[]{:S(2)}) collective-permute-start(bf16[2,64,768]{2,1,0:T(8,128)(2,1)S(1)} %select_select_fusion), channel_id=1, source_target_pairs={{0,4},{28,24},{1,5},{29,25},{2,6},{30,26},{3,7},{31,27}} | collective-permute-start | bytes 589832 | tf_op jit(solution)/shard_map/ppermute | solution.py:841
  28.9 61.6 %all-to-all-start = ((bf16[48,64,384]{2,1,0:T(8,128)(2,1)}), bf16[48,64,384]{2,1,0:T(8,128)(2,1)}, u32[]{:S(2)}, u32[]{:S(2)}) async-start(bf16[48,64,384]{2,1,0:T(8,128)(2,1)} %get-tuple-element.173), calls=%async_computation | async-start | bytes 4718592 | tf_op jit(solution)/shard_map/all_to_all | solution.py:873
  33.9 27.1 %collective-permute-start.4 = (bf16[2,64,384]{2,1,0:T(8,128)(2,1)}, bf16[2,64,384]{2,1,0:T(8,128)(2,1)S(1)}, u32[]{:S(2)}, u32[]{:S(2)}) collective-permute-start(bf16[2,64,384]{2,1,0:T(8,128)(2,1)} %get-tuple-element.169), channel_id=1, source_target_pairs={{0,4},{4,8},{8,12},{12,16},{16,20},{20,24},{24,28},{1,5},{5,9},{9,... | collective-permute-start | bytes 294920 | tf_op jit(solution)/shard_map/ppermute | solution.py:997
  37.8 23.2 %collective-permute-start.5 = (bf16[2,64,384]{2,1,0:T(8,128)(2,1)}, bf16[2,64,384]{2,1,0:T(8,128)(2,1)S(1)}, u32[]{:S(2)}, u32[]{:S(2)}) collective-permute-start(bf16[2,64,384]{2,1,0:T(8,128)(2,1)} %get-tuple-element.170), channel_id=1, source_target_pairs={{4,0},{8,4},{12,8},{16,12},{20,16},{24,20},{28,24},{5,1},{9,5},{13... | collective-permute-start | bytes 294920 | tf_op jit(solution)/shard_map/ppermute | solution.py:998
  52.6 43.7 %collective-permute-start.6 = (f32[2,64,256]{2,1,0:T(8,128)}, f32[2,64,256]{2,1,0:T(8,128)S(1)}, u32[]{:S(2)}, u32[]{:S(2)}) collective-permute-start(f32[2,64,256]{2,1,0:T(8,128)} %get-tuple-element.176), channel_id=1, source_target_pairs={{12,4},{20,16},{24,8},{28,0},{16,24},{8,12},{4,20},{0,28},{13,5},{... | collective-permute-start | bytes 393224 | tf_op jit(solution)/shard_map/ppermute | solution.py:857
  112.7 80.4 %all-to-all-start.1 = ((bf16[48,64,256]{2,1,0:T(8,128)(2,1)}), bf16[48,64,256]{2,1,0:T(8,128)(2,1)}, u32[]{:S(2)}, u32[]{:S(2)}) async-start(bf16[48,64,256]{2,1,0:T(8,128)(2,1)} %gather.1), calls=%async_computation.1 | async-start | bytes 3145728 | tf_op jit(solution)/shard_map/all_to_all | solution.py:873
  148.0 13.3 %collective-permute-start.25 = (bf16[128,768]{1,0:T(8,128)(2,1)S(1)}, bf16[128,768]{1,0:T(8,128)(2,1)S(1)}, u32[]{:S(2)}, u32[]{:S(2)}) collective-permute-start(bf16[128,768]{1,0:T(8,128)(2,1)S(1)} %get-tuple-element.220), channel_id=1, source_target_pairs={{0,1},{1,0},{2,3},{3,2},{4,5},{5,4},{6,7},{7,6},{8,9},{9,8},{10,11... | collective-permute-start | bytes 589832 | tf_op jit(solution)/shard_map/ppermute | solution.py:808
  149.8 11.5 %collective-permute-start.27 = (bf16[128,768]{1,0:T(8,128)(2,1)S(1)}, bf16[128,768]{1,0:T(8,128)(2,1)S(1)}, u32[]{:S(2)}, u32[]{:S(2)}) collective-permute-start(bf16[128,768]{1,0:T(8,128)(2,1)S(1)} %add_convert_fusion.4), channel_id=1, source_target_pairs={{0,2},{1,3},{2,0},{3,1},{4,6},{5,7},{6,4},{7,5},{8,10},{9,11},{10,... | collective-permute-start | bytes 589832 | tf_op jit(solution)/shard_map/ppermute | solution.py:808
  171.5 21.7 %collective-permute-start.38 = (bf16[4,96,768]{2,1,0:T(8,128)(2,1)S(1)}, bf16[4,96,768]{2,1,0:T(8,128)(2,1)}, u32[]{:S(2)}, u32[]{:S(2)}) collective-permute-start(bf16[4,96,768]{2,1,0:T(8,128)(2,1)S(1)} %get-tuple-element.257), channel_id=1, source_target_pairs={{0,4},{4,0},{8,12},{12,8},{16,20},{20,16},{24,28},{28,24},{1,5},{5... | collective-permute-start | bytes 1769480 | tf_op jit(solution)/shard_map/ppermute | solution.py:877
  193.1 45.3 %all-to-all-start.2 = ((bf16[48,64,256]{2,1,0:T(8,128)(2,1)}), bf16[48,64,256]{2,1,0:T(8,128)(2,1)}, u32[]{:S(2)}, u32[]{:S(2)}) async-start(bf16[48,64,256]{2,1,0:T(8,128)(2,1)} %get-tuple-element.258), calls=%async_computation.2 | async-start | bytes 3145728 | tf_op jit(solution)/shard_map/all_to_all | solution.py:873
  215.1 16.2 %collective-permute-start.41 = (bf16[2,64,640]{2,1,0:T(8,128)(2,1)}, bf16[2,64,640]{2,1,0:T(8,128)(2,1)S(1)}, u32[]{:S(2)}, u32[]{:S(2)}) collective-permute-start(bf16[2,64,640]{2,1,0:T(8,128)(2,1)} %get-tuple-element.265.given_ref), channel_id=1, source_target_pairs={{12,4},{20,16},{24,8},{28,0},{16,24},{8,12},{4,20},{0,28},{13,5},{... | collective-permute-start | bytes 491528 | tf_op jit(solution)/shard_map/ppermute | solution.py:857
  222.7 30.8 %collective-permute-start.46 = (bf16[4,96,768]{2,1,0:T(8,128)(2,1)S(1)}, bf16[4,96,768]{2,1,0:T(8,128)(2,1)}, u32[]{:S(2)}, u32[]{:S(2)}) collective-permute-start(bf16[4,96,768]{2,1,0:T(8,128)(2,1)S(1)} %get-tuple-element.277), channel_id=1, source_target_pairs={{0,4},{4,0},{8,12},{12,8},{16,20},{20,16},{24,28},{28,24},{1,5},{5... | collective-permute-start | bytes 1769480 | tf_op jit(solution)/shard_map/ppermute | solution.py:877
  232.4 23.6 %collective-permute-start.42 = (bf16[2,64,640]{2,1,0:T(8,128)(2,1)S(1)}, bf16[2,64,640]{2,1,0:T(8,128)(2,1)S(1)}, u32[]{:S(2)}, u32[]{:S(2)}) collective-permute-start(bf16[2,64,640]{2,1,0:T(8,128)(2,1)S(1)} %add_convert_fusion.8.refs_15_), channel_id=1, source_target_pairs={{4,0},{24,28},{5,1},{25,29},{6,2},{26,30},{7,3},{27,31}} | collective-permute-start | bytes 491528 | tf_op jit(solution)/shard_map/ppermute | solution.py:864
  233.7 22.3 %collective-permute-start.43 = (bf16[2,64,640]{2,1,0:T(8,128)(2,1)S(1)}, bf16[2,64,640]{2,1,0:T(8,128)(2,1)S(1)}, u32[]{:S(2)}, u32[]{:S(2)}) collective-permute-start(bf16[2,64,640]{2,1,0:T(8,128)(2,1)S(1)} %add_convert_fusion.8.refs_15_), channel_id=1, source_target_pairs={{8,0},{20,28},{9,1},{21,29},{10,2},{22,30},{11,3},{23,31}} | collective-permute-start | bytes 491528 | tf_op jit(solution)/shard_map/ppermute | solution.py:864
  235.0 21.0 %collective-permute-start.44 = (bf16[2,64,640]{2,1,0:T(8,128)(2,1)S(1)}, bf16[2,64,640]{2,1,0:T(8,128)(2,1)}, u32[]{:S(2)}, u32[]{:S(2)}) collective-permute-start(bf16[2,64,640]{2,1,0:T(8,128)(2,1)S(1)} %add_convert_fusion.8.refs_15_), channel_id=1, source_target_pairs={{16,0},{12,28},{17,1},{13,29},{18,2},{14,30},{19,3},{15,31}} | collective-permute-start | bytes 491528 | tf_op jit(solution)/shard_map/ppermute | solution.py:864
  256.0 40.0 %all-to-all-start.3 = ((bf16[4,96,1536]{2,1,0:T(8,128)(2,1)}), bf16[4,96,1536]{2,1,0:T(8,128)(2,1)}, u32[]{:S(2)}, u32[]{:S(2)}) async-start(bf16[4,96,1536]{2,1,0:T(8,128)(2,1)} %pad_maximum_fusion), calls=%async_computation.3 | async-start | bytes 2359296 | tf_op jit(solution)/shard_map/all_to_all | solution.py:898
  278.0 19.4 %collective-permute-start.45 = (bf16[4,96,896]{2,1,0:T(8,128)(2,1)}, bf16[4,96,896]{2,1,0:T(8,128)(2,1)}, u32[]{:S(2)}, u32[]{:S(2)}) collective-permute-start(bf16[4,96,896]{2,1,0:T(8,128)(2,1)} %get-tuple-element.273), channel_id=1, source_target_pairs={{0,4},{4,0},{8,12},{12,8},{16,20},{20,16},{24,28},{28,24},{1,5},{5... | collective-permute-start | bytes 2064392 | tf_op jit(solution)/shard_map/ppermute | solution.py:877
  278.0 32.2 %collective-permute-start.50 = (bf16[256,768]{1,0:T(8,128)(2,1)}, bf16[256,768]{1,0:T(8,128)(2,1)S(1)}, u32[]{:S(2)}, u32[]{:S(2)}) collective-permute-start(bf16[256,768]{1,0:T(8,128)(2,1)} %get-tuple-element.288), channel_id=1, source_target_pairs={{0,1},{1,0},{2,3},{3,2},{4,5},{5,4},{6,7},{7,6},{8,9},{9,8},{10,11... | collective-permute-start | bytes 1179656 | tf_op jit(solution)/shard_map/ppermute | solution.py:808
  278.1 21.8 %collective-permute-start.47 = (bf16[256,768]{1,0:T(8,128)(2,1)}, bf16[256,768]{1,0:T(8,128)(2,1)}, u32[]{:S(2)}, u32[]{:S(2)}) collective-permute-start(bf16[256,768]{1,0:T(8,128)(2,1)} %get-tuple-element.283), channel_id=1, source_target_pairs={{0,1},{1,0},{2,3},{3,2},{4,5},{5,4},{6,7},{7,6},{8,9},{9,8},{10,11... | collective-permute-start | bytes 1179656 | tf_op jit(solution)/shard_map/ppermute | solution.py:808
  280.1 30.1 %collective-permute-start.52 = (bf16[256,768]{1,0:T(8,128)(2,1)}, bf16[256,768]{1,0:T(8,128)(2,1)S(1)}, u32[]{:S(2)}, u32[]{:S(2)}) collective-permute-start(bf16[256,768]{1,0:T(8,128)(2,1)} %add_convert_fusion.2), channel_id=1, source_target_pairs={{0,2},{1,3},{2,0},{3,1},{4,6},{5,7},{6,4},{7,5},{8,10},{9,11},{10,... | collective-permute-start | bytes 1179656 | tf_op jit(solution)/shard_map/ppermute | solution.py:808
  283.5 18.8 %collective-permute-start.49 = (bf16[256,768]{1,0:T(8,128)(2,1)}, bf16[256,768]{1,0:T(8,128)(2,1)}, u32[]{:S(2)}, u32[]{:S(2)}) collective-permute-start(bf16[256,768]{1,0:T(8,128)(2,1)} %add_convert_fusion.3), channel_id=1, source_target_pairs={{0,2},{1,3},{2,0},{3,1},{4,6},{5,7},{6,4},{7,5},{8,10},{9,11},{10,... | collective-permute-start | bytes 1179656 | tf_op jit(solution)/shard_map/ppermute | solution.py:808
  299.6 12.4 %collective-permute-start.53 = (bf16[96,896]{1,0:T(8,128)(2,1)}, bf16[96,896]{1,0:T(8,128)(2,1)S(1)}, u32[]{:S(2)}, u32[]{:S(2)}) collective-permute-start(bf16[96,896]{1,0:T(8,128)(2,1)} %get-tuple-element.293), channel_id=1, source_target_pairs={{0,8},{4,12},{8,0},{12,4},{16,24},{20,28},{24,16},{28,20},{1,9},{5... | collective-permute-start | bytes 516104 | tf_op jit(solution)/shard_map/ppermute | solution.py:889
  299.9 15.7 %collective-permute-start.54 = (bf16[96,896]{1,0:T(8,128)(2,1)}, bf16[96,896]{1,0:T(8,128)(2,1)S(1)}, u32[]{:S(2)}, u32[]{:S(2)}) collective-permute-start(bf16[96,896]{1,0:T(8,128)(2,1)} %get-tuple-element.294), channel_id=1, source_target_pairs={{0,16},{4,20},{8,24},{12,28},{16,0},{20,4},{24,8},{28,12},{1,17},{... | collective-permute-start | bytes 516104 | tf_op jit(solution)/shard_map/ppermute | solution.py:889
  302.3 13.3 %collective-permute-start.55 = (bf16[96,896]{1,0:T(8,128)(2,1)}, bf16[96,896]{1,0:T(8,128)(2,1)S(1)}, u32[]{:S(2)}, u32[]{:S(2)}) collective-permute-start(bf16[96,896]{1,0:T(8,128)(2,1)} %get-tuple-element.295), channel_id=1, source_target_pairs={{0,24},{4,28},{8,16},{12,20},{16,8},{20,12},{24,0},{28,4},{1,25},{... | collective-permute-start | bytes 516104 | tf_op jit(solution)/shard_map/ppermute | solution.py:889
  (101 other events, 877.5 us)
